TPU v7x, 128 devices: a whole 4x4x4 slice. The times are simulated.
128 devices in a mesh: row: 8 (over z, y_hi), col: 16 (over x, y_lo, core).
Axes of the slice: x: 4, y: 4 (y_hi: 2, y_lo: 2; y = y_hi * 2 + y_lo), z: 4, core: 2. Of those that a mesh axis runs over, the one named last changes fastest.
Arguments:
- context_frames: bfloat16 [4, 768, 4096], P(None, 'row', 'col'), may hold values from -6 to 6
- latent_noise: bfloat16 [48, 256, 8], P('row', 'col'), may hold values from -6 to 6
- latent_proj: bfloat16 [8, 384], replicated, may hold values from -2 to 2
- coarse_context: bfloat16 [1024, 384], replicated, may hold values from -0.1875 to 0.1875
- fine_context: bfloat16 [256, 192], replicated, may hold values from -0.375 to 0.375
- coarse_gates: bfloat16 [6912, 768], replicated, may hold values from -0.078125 to 0.078125
- coarse_candidate: bfloat16 [6912, 384], replicated, may hold values from -0.078125 to 0.078125
- fine_gates: bfloat16 [3456, 384], replicated, may hold values from -0.109375 to 0.109375
- fine_candidate: bfloat16 [3456, 192], replicated, may hold values from -0.109375 to 0.109375
- upsample_proj: bfloat16 [384, 768], replicated, may hold values from -0.3125 to 0.3125
- head_proj: bfloat16 [192, 64], replicated, may hold values from -0.4375 to 0.4375
Outputs:
- forecast: float32 [2, 768, 4096], P(None, 'row', 'col')
All inputs are finite; a program needn't handle non-finite values.
Results may differ from a plain program's by a relative error of at most 0.0055.
Values may be sent and summed in bfloat16 or wider, within the bound.
No kernel may reach another device: no remote copies, remote signals or barrier semaphores. Data moves between devices by JAX's collectives and lax.ppermute only.
A program may use at most 128 MiB of HBM per device.

v0:
```python
import functools

import jax
import jax.numpy as jnp
from jax import lax
from jax.experimental import pallas as pl
from jax.experimental.pallas import tpu as pltpu
from jax.sharding import PartitionSpec as P

F32 = jnp.float32
BF16 = jnp.bfloat16

C2, C1 = 384, 192
GRID_ROWS, GRID_COLS = 48, 256
RC, CC = 6, 16
RF, CF = 12, 32
HC, HF = 5, 4
EC, EF = RC + 2 * HC, RF + 2 * HF
PC, PF = 32, 48
QC, QF = 24, 40
ROW_BUF, COL_BUF = 160, 144
TAPS = 9
KC = TAPS * C2 + 128

VMEM = pl.BlockSpec(memory_space=pltpu.VMEM)
SMEM = pl.BlockSpec(memory_space=pltpu.SMEM)
ANY = pl.BlockSpec(memory_space=pl.ANY)
HBM = pl.BlockSpec(memory_space=pltpu.HBM)


def dot(a, b):
    return jnp.dot(a, b, preferred_element_type=F32)


def dot_t(a, b):
    return lax.dot_general(a, b, (((1,), (1,)), ((), ())), preferred_element_type=F32)


def sigmoid(x):
    return 0.5 * jnp.tanh(0.5 * x) + 0.5


def iota(shape, dim):
    return lax.broadcasted_iota(jnp.int32, shape, dim)


def tiles_get(ref, rows):
    return jnp.concatenate([ref[t, rows, :] for t in range(ref.shape[0])], 1)


def tiles_put(ref, rows, value):
    lanes = ref.shape[0] * 128
    if value.shape[1] < lanes:
        value = jnp.concatenate([value, jnp.zeros((value.shape[0], lanes - value.shape[1]), F32)], 1)
    for t in range(ref.shape[0]):
        ref[t, rows, :] = value[:, 128 * t : 128 * t + 128]


def indicator(cond):
    return jnp.where(cond, 1.0, 0.0).astype(BF16)


def start_kernel(
    place,
    frames_hbm,
    noise_hbm,
    context2_hbm,
    context1_hbm,
    hc_out,
    hf_out,
    noise_out,
    even_out,
    odd_out,
    frames,
    noise,
    context2,
    context1,
    buf,
    sem,
):
    moves = [
        pltpu.make_async_copy(src, dst, sem.at[i])
        for i, (src, dst) in enumerate(
            ((frames_hbm, frames), (context2_hbm, context2), (context1_hbm, context1), (noise_hbm, noise))
        )
    ]
    for copy in moves:
        copy.start()

    def pick(shift, parity):
        row, col = iota((128, 256), 0), iota((128, 256), 1)
        count = 256 >> shift
        j = 2 * (row >> (8 - shift)) + parity
        return indicator(col == ((row & (count - 1)) << shift) + j)

    moves[0].wait()
    zeros = jnp.zeros((64, 256), BF16)
    even, odd = [], []
    for r in range(RC):
        band = frames[:, 16 * r : 16 * r + 16, :].reshape(64, 256)
        even += [band, zeros]
        odd += [zeros, band]
    even, odd = jnp.concatenate(even, 0), jnp.concatenate(odd, 0)

    def turned(shift):
        both = dot_t(pick(shift, 0), even) + dot_t(pick(shift, 1), odd)
        return both.astype(BF16)

    deep = turned(4)
    left = jnp.concatenate(
        [
            jnp.concatenate([deep[16 * j : 16 * j + 16, 128 * r : 128 * r + 128] for r in range(RC)], 0)
            for j in range(8)
        ],
        1,
    )
    row, col = iota((256, 256), 0), iota((256, 256), 1)
    swap = indicator(col == ((row & 15) << 4) + (row >> 4))
    moves[1].wait()
    moved = [dot(swap, context2[256 * f : 256 * f + 256, :]).astype(BF16) for f in range(4)]
    weight = jnp.concatenate([moved[f][16 * j : 16 * j + 16] for j in range(16) for f in range(4)], 0)
    state2 = jnp.tanh(dot(left, weight))
    hc_out[...] = state2.astype(BF16).reshape(RC, CC, C2)

    deep = turned(3)
    left = jnp.concatenate(
        [
            jnp.concatenate([deep[32 * j : 32 * j + 32, 128 * r : 128 * r + 128] for r in range(RC)], 0)
            for j in range(4)
        ],
        1,
    )
    row, col = iota((512, 256), 0), iota((512, 256), 1)
    moves[2].wait()
    source = (((row >> 4) & 3) << 6) + ((row & 7) << 3) + (row >> 6)
    for q in range(2):
        spread = indicator((col == source) & (((row >> 3) & 1) == q))
        weight = dot_t(spread, context1[...]).astype(BF16)
        state1 = jnp.tanh(dot(left, weight)).astype(BF16)
        for r in range(RC):
            hf_out[2 * r + q] = state1[CF * r : CF * r + CF]

    moves[3].wait()
    diagonal = indicator(iota((16, 16), 0) == iota((16, 16), 1))
    turned_noise = dot_t(diagonal, noise[...].reshape(RC * 8, CC))
    turned_noise = jnp.concatenate([turned_noise, jnp.zeros((16, 128 - 8 * RC), F32)], 1)
    noise_out[...] = turned_noise.astype(BF16)
    low_noise = pltpu.roll(turned_noise, 128 - 8 * (RC - HC), 1)

    up_first = (place[0] & 1) == 1
    for target, up in ((even_out, up_first), (odd_out, jnp.logical_not(up_first))):
        c_top = state2[: HC * CC]
        c_low = state2[(RC - HC) * CC :]
        buf[0:80, :] = jnp.where(up, c_top, c_low)
        for half in range(2):
            f_top = hf_out[2 * half : 2 * half + 2].reshape(64, C1).astype(F32)
            f_low = hf_out[RF - HF + 2 * half : RF - HF + 2 * half + 2].reshape(64, C1).astype(F32)
            buf[80:144, C1 * half : C1 * half + C1] = jnp.where(up, f_top, f_low)
        buf[144:160, :] = jnp.zeros((16, C2), F32)
        buf[144:160, 0:128] = jnp.where(up, turned_noise, low_noise)
        target[...] = buf[...].astype(BF16)


def column_kernel(
    place, hc, hf, noise, even_in, odd_in, after, ec_out, ef_out, en_out, even_out, odd_out, sc, sf, sn, buf
):
    up_first = (place[0] & 1) == 1
    above = jnp.where(up_first, even_in[...].astype(F32), odd_in[...].astype(F32))
    below = jnp.where(up_first, odd_in[...].astype(F32), even_in[...].astype(F32))
    tiles_put(sc, pl.ds(0, 80), above[0:80])
    tiles_put(sc, pl.ds(80, 96), hc[...].reshape(RC * CC, C2).astype(F32))
    tiles_put(sc, pl.ds(176, 80), below[0:80])
    for half in range(2):
        tiles_put(sf, pl.ds(64 * half, 64), above[80:144, C1 * half : C1 * half + C1])
        tiles_put(sf, pl.ds(512 + 64 * half, 64), below[80:144, C1 * half : C1 * half + C1])
    tiles_put(sf, pl.ds(128, 384), hf[...].reshape(RF * CF, C1).astype(F32))
    tiles_put(sf, pl.ds(640, 128), jnp.zeros((128, C1), F32))
    sn[...] = jnp.zeros(sn.shape, F32)
    for h in range(HC):
        sn[16 * h : 16 * h + 16, 0:8] = above[144:160, 8 * h : 8 * h + 8]
        sn[16 * (HC + RC + h) : 16 * (HC + RC + h) + 16, 0:8] = below[144:160, 8 * h : 8 * h + 8]
    for h in range(RC):
        sn[16 * (HC + h) : 16 * (HC + h) + 16, 0:8] = noise[:, 8 * h : 8 * h + 8].astype(F32)

    ec_out[...] = tiles_get(sc, pl.ds(0, EC * CC)).astype(BF16).reshape(EC, CC, C2)
    ef_out[...] = tiles_get(sf, pl.ds(0, EF * CF))[:, :C1].astype(BF16).reshape(EF, CF, C1)
    en_out[...] = sn[...].astype(BF16).reshape(EC, CC, 128)

    left_first = (place[1] & 1) == 1
    for target, left in ((even_out, left_first), (odd_out, jnp.logical_not(left_first))):
        c_from = jnp.where(left, 0, CC - HC)
        f_from = jnp.where(left, 0, CF - HF)
        buf[128:144, :] = jnp.zeros((16, C2), F32)
        for k in range(HC):
            buf[16 * k : 16 * k + 16, :] = tiles_get(sc, pl.ds(c_from + k, 16, stride=CC))
            strip = sn[pl.ds(c_from + k, 16, stride=CC), :]
            buf[128:144, 8 * k : 8 * k + 8] = strip[:, 0:8]
        for k in range(HF):
            at, lane = 80 + 24 * (k % 2), C1 * (k // 2)
            buf[at : at + 24, lane : lane + C1] = tiles_get(sf, pl.ds(f_from + k, 24, stride=CF))[:, :C1]
        target[...] = buf[...].astype(BF16)


def coarse_weights_kernel(
    proj_hbm, gates_hbm, cand_hbm, wg_out, wc_out, token, proj, gates, cand, acc_g, acc_c, sem
):
    count = [0]

    def move(src, dst):
        copy = pltpu.make_async_copy(src, dst, sem.at[count[0]])
        count[0] += 1
        copy.start()
        return copy

    first = move(proj_hbm, proj)
    inputs, states = [], []
    for hbm, held in ((gates_hbm, gates), (cand_hbm, cand)):
        inputs.append([move(hbm.at[pl.ds(2 * C2 * t, C2), :], held.at[t]) for t in range(TAPS)])
    for hbm, target in ((gates_hbm, wg_out), (cand_hbm, wc_out)):
        for t in range(TAPS):
            states.append(move(hbm.at[pl.ds(2 * C2 * t + C2, C2), :], target.at[pl.ds(C2 * t, C2), :]))
    acc_g[...] = jnp.zeros(acc_g.shape, F32)
    acc_c[...] = jnp.zeros(acc_c.shape, F32)
    first.wait()
    token[...] = jnp.zeros(token.shape, F32)
    wide = jnp.concatenate([proj[...].astype(F32), jnp.zeros((8, C2), F32)], 0).astype(BF16)
    for copies, held, acc in ((inputs[0], gates, acc_g), (inputs[1], cand, acc_c)):
        for t in range(TAPS):
            copies[t].wait()
            acc[8 * t : 8 * t + 8, :] = dot(wide, held[t])[0:8]
    wg_out[TAPS * C2 :, :] = acc_g[...].astype(BF16)
    wc_out[TAPS * C2 :, :] = acc_c[...].astype(BF16)
    for copy in states:
        copy.wait()


def fine_weights_kernel(
    after, gates_hbm, cand_hbm, up_hbm, head_hbm, wg_out, wc_out, up_out, head_out, up, head, sem
):
    moves = [
        pltpu.make_async_copy(src, dst, sem.at[i])
        for i, (src, dst) in enumerate(
            ((up_hbm, up), (head_hbm, head), (gates_hbm, wg_out), (cand_hbm, wc_out))
        )
    ]
    for copy in moves:
        copy.start()
    moves[1].wait()
    row, col = iota((2048, 64), 0), iota((2048, 64), 1)
    spread = indicator(col == ((row >> 8) << 3) + (row & 7))
    head_out[...] = dot(spread, head[...]).astype(BF16)
    moves[0].wait()
    wide = up[...].astype(F32)
    zeros = jnp.zeros((C2, 256 - C1), F32)
    for i in range(4):
        part = jnp.concatenate([wide[:, C1 * i : C1 * i + C1], zeros], 1)
        up_out[:, 256 * i : 256 * i + 256] = part.astype(BF16)
    moves[2].wait()
    moves[3].wait()


def main_kernel(
    place,
    ec,
    ef,
    en,
    even_in,
    odd_in,
    wg2,
    wc2,
    wg1,
    wc1,
    wup,
    whead,
    out,
    sc,
    sf,
    xf,
    hf,
    sn,
    patch,
    gate_u,
    reset_h,
    next_h,
    gate_uf,
    copies,
    frame,
):
    row0, col0 = place[0], place[1]
    left_first = (col0 & 1) == 1
    left = jnp.where(left_first, even_in[...].astype(F32), odd_in[...].astype(F32))
    right = jnp.where(left_first, odd_in[...].astype(F32), even_in[...].astype(F32))

    xf[...] = jnp.zeros(xf.shape, F32)
    hf[...] = jnp.zeros(hf.shape, F32)
    sn[...] = jnp.zeros(sn.shape, F32)
    patch[...] = jnp.zeros(patch.shape, F32)
    gate_u[...] = jnp.zeros(gate_u.shape, F32)
    reset_h[...] = jnp.zeros(reset_h.shape, F32)
    next_h[...] = jnp.zeros(next_h.shape, F32)
    gate_uf[...] = jnp.zeros(gate_uf.shape, F32)
    for h in range(EC):
        tiles_put(sc, pl.ds(PC * h + 8, CC), ec[h].astype(F32))
        sn[PC * h + 8 : PC * h + 24, :] = en[h].astype(F32)
    for k in range(HC):
        for side, at in ((left, 8 - HC + k), (right, 8 + CC + k)):
            tiles_put(sc, pl.ds(at, EC, stride=PC), side[16 * k : 16 * k + 16])
            strip = jnp.concatenate([side[128:144, 8 * k : 8 * k + 8], jnp.zeros((16, 120), F32)], 1)
            sn[pl.ds(at, EC, stride=PC), :] = strip
    for h in range(EF):
        tiles_put(hf, pl.ds(PF * h + 8, CF), ef[h].astype(F32))
    for k in range(HF):
        at, lane = 80 + 24 * (k % 2), C1 * (k // 2)
        for side, col in ((left, 8 - HF + k), (right, 8 + CF + k)):
            tiles_put(hf, pl.ds(col, EF, stride=PF), side[at : at + EF, lane : lane + C1])
    sf[:, C1 : 2 * C1] = tiles_get(hf, pl.ds(0, EF * PF))[:, :C1]

    noise = sn[...].reshape(EC, PC, 128)
    total = None
    for dx in range(3):
        part = None
        for dy in range(3):
            moved = noise[dy : dy + EC - 2]
            if dy or dx:
                moved = pltpu.roll(moved, 8 * (3 * dy + dx), 2)
            part = moved if part is None else part + moved
        part = part[:, 3 + dx : 3 + dx + QC, :]
        total = part if total is None else total + part
    patch[:, 0:QC, :] = total

    def spread(field, width, pitch, lanes, rows_out, narrow):
        for dx in range(3):
            moved = field(dx)
            rows = rows_out + 2
            copies[dx, 0 : rows * pitch, 0:lanes] = moved.reshape(rows * pitch, lanes).astype(BF16)
            if narrow:
                inner = moved[1 : 1 + rows_out].reshape(rows_out * pitch, lanes)
                copies[3 + dx, 0 : rows_out * pitch, 0:lanes] = inner.astype(BF16)
        parts = []
        for dy in range(3):
            for dx in range(3):
                if dy == 1 and narrow:
                    parts.append(copies[3 + dx, 0 : rows_out * pitch, 0:lanes])
                else:
                    parts.append(copies[dx, dy * pitch : (dy + rows_out) * pitch, 0:lanes])
        return parts

    def coarse_conv(field, rows_out, offset, weight):
        parts = spread(field, C2, QC, C2, rows_out, True)
        near = patch[offset : offset + rows_out, offset : offset + QC, :]
        parts.append(near.reshape(rows_out * QC, 128).astype(BF16))
        return dot(jnp.concatenate(parts, 1), weight[...])

    def inside(shape, row_from, row_end, col_from, col_end):
        row = iota(shape, 0) + row_from
        col = iota(shape, 1) + col_from
        return (row >= 0) & (row < row_end) & (col >= 0) & (col < col_end)

    def coarse_step(step, read):
        rows = 14 - 4 * step
        gates = coarse_conv(lambda dx: read(0, dx, rows + 2, QC), rows, 2 * step, wg2)
        reset_h[0:rows, 0:QC, :] = sigmoid(gates[:, :C2]).reshape(rows, QC, C2) * read(1, 1, rows, QC)
        gate_u[0:rows, 0:QC, :] = sigmoid(gates[:, C2:]).reshape(rows, QC, C2)
        cand = jnp.tanh(
            coarse_conv(lambda dx: reset_h[0:rows, dx : dx + QC, :], rows - 2, 2 * step + 1, wc2)
        ).reshape(rows - 2, QC, C2)
        update = gate_u[1 : rows - 1, 1 : 1 + QC, :]
        state = update * read(2, 2, rows - 2, QC) + (1.0 - update) * cand
        first = 2 + 2 * step
        valid = inside(state.shape, row0 * RC + first - HC, GRID_ROWS, col0 * CC + first - HC, GRID_COLS)
        return jnp.where(valid, state, 0.0).astype(BF16)

    def fine_input(state, rows, row_to, col_to):
        value = dot(state.reshape(rows * QC, C2), wup[...])
        for q in range(2):
            for p in range(2):
                lane = 256 * (2 * q + p)
                for r in range(rows):
                    at = (row_to + 2 * r + q) * PF + col_to + p
                    tiles_put(xf, pl.ds(at, QC, stride=2), value[QC * r : QC * r + QC, lane : lane + 256])
        sf[:, 0:C1] = tiles_get(xf, pl.ds(0, EF * PF))[:, :C1]

    def fine_step(step):
        rows = 18 - 4 * step
        first = 2 * step
        field = sf[...].reshape(EF, PF, 2 * C1)
        parts = spread(
            lambda dx: field[first : first + rows + 2, 4 + first + dx : 4 + first + dx + QF, :],
            2 * C1, QF, 2 * C1, rows, True,
        )
        gates = dot(jnp.concatenate(parts, 1), wg1[...])
        reset = sigmoid(gates[:, :C1]).reshape(rows, QF, C1)
        state = tiles_get(hf, pl.ds(0, EF * PF))[:, :C1].reshape(EF, PF, C1)
        near = reset * state[first + 1 : first + 1 + rows, 5 + first : 5 + first + QF, :]
        gate_uf[0:rows, 0:QF, :] = sigmoid(gates[:, C1:]).reshape(rows, QF, C1)
        for r in range(rows):
            at = (first + 1 + r) * PF + 5 + first
            sf[at : at + QF, C1 : 2 * C1] = near[r]
        field = sf[...].reshape(EF, PF, 2 * C1)
        width = CF if step else QF
        parts = spread(
            lambda dx: field[first + 1 : first + 1 + rows, 5 + first + dx : 5 + first + dx + width, :],
            2 * C1, width, 2 * C1, rows - 2, width % 16 != 0,
        )
        cand = jnp.tanh(dot_t(jnp.concatenate(parts, 1), wc1[...])).reshape(rows - 2, width, C1)
        update = gate_uf[1 : rows - 1, 1 : 1 + width, :]
        old = state[first + 2 : first + rows, 6 + first : 6 + first + width, :]
        new = update * old + (1.0 - update) * cand
        if step == 0:
            valid = inside(
                new.shape, row0 * RF + 2 - HF, 2 * GRID_ROWS, col0 * CF + 2 - HF, 2 * GRID_COLS
            )
            new = jnp.where(valid, new, 0.0).astype(BF16).astype(F32)
            for r in range(rows - 2):
                at = (2 + r) * PF + 6
                tiles_put(hf, pl.ds(at, QF), new[r])
                sf[at : at + QF, C1 : 2 * C1] = new[r]
            return new[2:14, 2 : 2 + CF, :].reshape(RF * CF, C1).astype(BF16)
        return new.reshape(RF * CF, C1).astype(BF16)

    def emit(step, state):
        mask = (iota((RF, CF, 256), 2) >> 3) == iota((RF, CF, 256), 1)
        for r in range(8):
            value = dot_t(state, whead[256 * r : 256 * r + 256, :]).reshape(RF, CF, 256)
            tiles_put(frame, pl.ds(r, RF, stride=8), jnp.sum(jnp.where(mask, value, 0.0), axis=1))
        out[step] = tiles_get(frame, pl.ds(0, 8 * RF))

    field2 = tiles_get(sc, pl.ds(0, EC * PC)).reshape(EC, PC, C2)
    state2 = coarse_step(0, lambda r, c, rows, cols: field2[r : r + rows, 3 + c : 3 + c + cols, :])
    next_h[:, 0:QC, :] = state2.astype(F32)
    fine_input(state2[1:11], 10, 0, 2)
    state1 = fine_step(0)
    emit(0, state1)
    state2 = coarse_step(1, lambda r, c, rows, cols: next_h[r : r + rows, c : c + cols, :])
    fine_input(state2, 8, 2, 6)
    emit(1, fine_step(1))


def in_hbm(value):
    return pltpu.with_memory_space_constraint(value, pltpu.HBM)


def swapped(value, axis, odd):
    pairs = []
    for i in range(odd, lax.axis_size(axis) - 1, 2):
        pairs += [(i, i + 1), (i + 1, i)]
    return lax.ppermute(value, axis, pairs)


def call(kernel, out_shape, in_specs, scratch, limit, flops, bytes_accessed, **extra):
    return pl.pallas_call(
        kernel,
        out_shape=out_shape,
        in_specs=in_specs,
        out_specs=[VMEM] * len(out_shape),
        scratch_shapes=scratch,
        compiler_params=pltpu.CompilerParams(vmem_limit_bytes=limit),
        cost_estimate=pl.CostEstimate(flops=flops, bytes_accessed=bytes_accessed, transcendentals=0),
        **extra,
    )


def on_device(
    context_frames,
    latent_noise,
    latent_proj,
    coarse_context,
    fine_context,
    coarse_gates,
    coarse_candidate,
    fine_gates,
    fine_candidate,
    upsample_proj,
    head_proj,
):
    place = jnp.stack([lax.axis_index("row"), lax.axis_index("col")]).astype(jnp.int32)
    shape = jax.ShapeDtypeStruct
    row_buf, col_buf = shape((ROW_BUF, C2), BF16), shape((COL_BUF, C2), BF16)

    hc, hf, noise, even, odd = call(
        start_kernel,
        [
            shape((RC, CC, C2), BF16),
            shape((RF, CF, C1), BF16),
            shape((16, 128), BF16),
            row_buf,
            row_buf,
        ],
        [SMEM] + [HBM] * 4,
        [
            pltpu.VMEM((4, 16 * RC, 16 * CC), BF16),
            pltpu.VMEM((RC, 8, CC), BF16),
            pltpu.VMEM((1024, C2), BF16),
            pltpu.VMEM((C1, 256), BF16),
            pltpu.VMEM((ROW_BUF, C2), F32),
            pltpu.SemaphoreType.DMA((4,)),
        ],
        16 << 20, 10**9, 2 << 20,
    )(
        place,
        in_hbm(context_frames),
        in_hbm(latent_noise.transpose(0, 2, 1)),
        in_hbm(coarse_context),
        in_hbm(fine_context.T),
    )

    even, odd = swapped(even, "row", 0), swapped(odd, "row", 1)

    wg2, wc2, token = call(
        coarse_weights_kernel,
        [shape((KC, 2 * C2), BF16), shape((KC, C2), BF16), shape((8, 128), F32)],
        [HBM] * 3,
        [
            pltpu.VMEM((8, C2), BF16),
            pltpu.VMEM((TAPS, C2, 2 * C2), BF16),
            pltpu.VMEM((TAPS, C2, C2), BF16),
            pltpu.VMEM((128, 2 * C2), F32),
            pltpu.VMEM((128, C2), F32),
            pltpu.SemaphoreType.DMA((4 * TAPS + 1,)),
        ],
        16 << 20, 10**9, 24 << 20,
    )(in_hbm(latent_proj), in_hbm(coarse_gates), in_hbm(coarse_candidate))

    ec, ef, en, even, odd = call(
        column_kernel,
        [
            shape((EC, CC, C2), BF16),
            shape((EF, CF, C1), BF16),
            shape((EC, CC, 128), BF16),
            col_buf,
            col_buf,
        ],
        [SMEM] + [VMEM] * 5 + [ANY],
        [
            pltpu.VMEM((3, EC * CC, 128), F32),
            pltpu.VMEM((2, 24 * CF, 128), F32),
            pltpu.VMEM((EC * CC, 128), F32),
            pltpu.VMEM((COL_BUF, C2), F32),
        ],
        8 << 20, 10**6, 2 << 20,
    )(place, hc, hf, noise, even, odd, token)

    even, odd = swapped(even, "col", 0), swapped(odd, "col", 1)

    wg1, wc1, up, head = call(
        fine_weights_kernel,
        [
            shape((18 * C1, 2 * C1), BF16),
            shape((C1, 18 * C1), BF16),
            shape((C2, 1024), BF16),
            shape((2048, C1), BF16),
        ],
        [ANY] + [HBM] * 4,
        [
            pltpu.VMEM((C2, 4 * C1), BF16),
            pltpu.VMEM((64, C1), BF16),
            pltpu.SemaphoreType.DMA((4,)),
        ],
        8 << 20, 10**8, 8 << 20,
    )(en, in_hbm(fine_gates), in_hbm(fine_candidate.T), in_hbm(upsample_proj), in_hbm(head_proj.T))

    (forecast,) = call(
        main_kernel,
        [shape((2, 96, 256), F32)],
        [SMEM] + [VMEM] * 11,
        [
            pltpu.VMEM((3, EC * PC, 128), F32),
            pltpu.VMEM((EF * PF, 2 * C1), F32),
            pltpu.VMEM((2, EF * PF + 16, 128), F32),
            pltpu.VMEM((2, EF * PF, 128), F32),
            pltpu.VMEM((EC * PC, 128), F32),
            pltpu.VMEM((EC - 2, PC, 128), F32),
            pltpu.VMEM((14, PC, C2), F32),
            pltpu.VMEM((14, PC, C2), F32),
            pltpu.VMEM((12, PC, C2), F32),
            pltpu.VMEM((18, PF, C1), F32),
            pltpu.VMEM((6, EF * QF, 2 * C1), BF16),
            pltpu.VMEM((2, 8 * RF, 128), F32),
        ],
        40 << 20, 9 * 10**9, 30 << 20,
    )(place, ec, ef, en, even, odd, wg2, wc2, wg1, wc1, up, head)
    return forecast


def solution(mesh):
    return jax.shard_map(
        on_device,
        mesh=mesh,
        in_specs=(
            P(None, "row", "col"),
            P("row", "col", None),
            P(),
            P(),
            P(),
            P(),
            P(),
            P(),
            P(),
            P(),
            P(),
        ),
        out_specs=P(None, "row", "col"),
        check_vma=False,
    )
```

profile of v0, /device:TPU:19, one launch (start us, length us, event | category | flops | bytes accessed | tf_op | source)
XLA Modules:
  0.0 51.0 jit_solution(14282329832285290927)
XLA Ops:
  0.0 0.1 pad_add_fusion.place
  0.1 3.7 %shard_map.109 = (bf16[6,16,384]{2,1,0:T(8,128)(2,1)S(1)}, bf16[12,32,192]{2,1,0:T(8,128)(2,1)S(1)}, bf16[16,128]{1,0:T(8,128)(2,1)S(1)}, bf16[160,384]{1,0:T(8,128)(2,1)S(1)}, bf16[160,384]{1,0:T(8,128)(2,1)S(1)}) custom-call(s32[2]{0:T(128)S(1)} %pad_add_fusion.place, bf16[4,96,256]{2,1,0:T(8,128)(2,1)} %frames_hbm.1, bf16[6,8,16]{2,1,0:T(8,128)(2,1)} %bitcast.9, ...), custom_call_target="tpu_custom_call" | custom-call | flops 1000000000 | bytes 2097152 | tf_op jit(solution)/shard_map/pallas_call | solution.py:480
  3.8 0.1 collective-permute-start
  4.0 6.2 %collective-permute-start.1 = (bf16[160,384]{1,0:T(8,128)(2,1)S(1)}, bf16[160,384]{1,0:T(8,128)(2,1)S(1)}, u32[]{:S(2)}, u32[]{:S(2)}) collective-permute-start(bf16[160,384]{1,0:T(8,128)(2,1)S(1)} %get-tuple-element.26), channel_id=1, source_target_pairs={{16,32},{32,16},{48,64},{64,48},{80,96},{96,80},{17,33},{33,17},{4... | collective-permute-start | bytes 368648 | tf_op jit(solution)/shard_map/ppermute | solution.py:447
  10.1 5.8 %shard_map.110 = (bf16[3584,768]{1,0:T(8,128)(2,1)S(1)}, bf16[3584,384]{1,0:T(8,128)(2,1)S(1)}, f32[8,128]{1,0:T(8,128)S(1)}) custom-call(bf16[8,384]{1,0:T(8,128)(2,1)} %proj_hbm.1, bf16[6912,768]{1,0:T(8,128)(2,1)} %gates_hbm.2, bf16[6912,384]{1,0:T(8,128)(2,1)} %cand_hbm.1), custom_call_target="tpu_custom_call" | custom-call | flops 1000000000 | bytes 25165824 | tf_op jit(solution)/shard_map/pallas_call | solution.py:509
  16.0 0.0 copy-start
  16.0 2.4 %copy-done = bf16[3584,768]{1,0:T(8,128)(2,1)} copy-done((bf16[3584,768]{1,0:T(8,128)(2,1)}, bf16[3584,768]{1,0:T(8,128)(2,1)S(1)}, u32[]{:S(2)}) %copy-start) | copy-done | bytes 5505048
  18.4 0.0 collective-permute-done.even_in
  18.4 0.0 collective-permute-done.1.odd_in
  18.4 1.0 %shard_map.111 = (bf16[16,16,384]{2,1,0:T(8,128)(2,1)S(1)}, bf16[20,32,192]{2,1,0:T(8,128)(2,1)S(1)}, bf16[16,16,128]{2,1,0:T(8,128)(2,1)S(1)}, bf16[144,384]{1,0:T(8,128)(2,1)S(1)}, bf16[144,384]{1,0:T(8,128)(2,1)S(1)}) custom-call(s32[2]{0:T(128)S(1)} %pad_add_fusion.place, bf16[6,16,384]{2,1,0:T(8,128)(2,1)S(1)} %get-tuple-element.22.hc, ...), custom_call_target="tpu_custom_call" | custom-call | flops 1000000 | bytes 2097152 | tf_op jit(solution)/shard_map/pallas_call | solution.py:524
  19.4 1.3 %collective-permute-start.2 = (bf16[144,384]{1,0:T(8,128)(2,1)S(1)}, bf16[144,384]{1,0:T(8,128)(2,1)S(1)}, u32[]{:S(2)}, u32[]{:S(2)}) collective-permute-start(bf16[144,384]{1,0:T(8,128)(2,1)S(1)} %get-tuple-element.31), channel_id=1, source_target_pairs={{0,1},{1,0},{2,3},{3,2},{4,5},{5,4},{6,7},{7,6},{8,9},{9,8},{10,11... | collective-permute-start | bytes 331784 | tf_op jit(solution)/shard_map/ppermute | solution.py:447
  20.8 3.0 %collective-permute-start.3 = (bf16[144,384]{1,0:T(8,128)(2,1)S(1)}, bf16[144,384]{1,0:T(8,128)(2,1)S(1)}, u32[]{:S(2)}, u32[]{:S(2)}) collective-permute-start(bf16[144,384]{1,0:T(8,128)(2,1)S(1)} %get-tuple-element.32), channel_id=1, source_target_pairs={{1,2},{2,1},{3,4},{4,3},{5,6},{6,5},{7,8},{8,7},{9,10},{10,9},{11,... | collective-permute-start | bytes 331784 | tf_op jit(solution)/shard_map/ppermute | solution.py:447
  23.8 2.4 %shard_map.112 = (bf16[3456,384]{1,0:T(8,128)(2,1)S(1)}, bf16[192,3456]{1,0:T(8,128)(2,1)S(1)}, bf16[384,1024]{1,0:T(8,128)(2,1)S(1)}, bf16[2048,192]{1,0:T(8,128)(2,1)S(1)}) custom-call(bf16[16,16,128]{2,1,0:T(8,128)(2,1)S(1)} %get-tuple-element.30.after.en, bf16[3456,384]{1,0:T(8,128)(2,1)} %gates_hbm.3, bf16[192,3456]{1,0:T(8,128)(2,1)} %bitcast.6, ...), custom_call_target="tpu_custom_call" | custom-call | flops 100000000 | bytes 8388608 | tf_op jit(solution)/shard_map/pallas_call | solution.py:545
  26.1 0.0 collective-permute-done.2.even_in
  26.1 1.9 %collective-permute-done.3.odd_in = bf16[144,384]{1,0:T(8,128)(2,1)S(1)} collective-permute-done((bf16[144,384]{1,0:T(8,128)(2,1)S(1)}, bf16[144,384]{1,0:T(8,128)(2,1)S(1)}, u32[]{:S(2)}, u32[]{:S(2)}) %collective-permute-start.3) | collective-permute-done | bytes 110624 | tf_op jit(solution)/shard_map/ppermute | solution.py:447
  28.0 23.0 %shard_map.113 = f32[2,96,256]{2,1,0:T(8,128)} custom-call(s32[2]{0:T(128)S(1)} %pad_add_fusion.place, bf16[16,16,384]{2,1,0:T(8,128)(2,1)S(1)} %get-tuple-element.28.ec, bf16[20,32,192]{2,1,0:T(8,128)(2,1)S(1)} %get-tuple-element.29.ef, bf16[16,16,128]{2,1,0:T(8,128)(2,1)S(1)} %get-tuple-element.30.after.en, ...), custom_call_target="tpu_custom_call" | custom-call | flops 8999999488 | bytes 31457280 | tf_op jit(solution)/shard_map/pallas_call | solution.py:562
Async XLA Ops:
  3.8 14.6 %collective-permute-start = (bf16[160,384]{1,0:T(8,128)(2,1)S(1)}, bf16[160,384]{1,0:T(8,128)(2,1)S(1)}, u32[]{:S(2)}, u32[]{:S(2)}) collective-permute-start(bf16[160,384]{1,0:T(8,128)(2,1)S(1)} %get-tuple-element.25), channel_id=1, source_target_pairs={{0,16},{16,0},{32,48},{48,32},{64,80},{80,64},{96,112},{112,96},{1... | collective-permute-start | bytes 368648 | tf_op jit(solution)/shard_map/ppermute | solution.py:447
  4.0 14.5 %collective-permute-start.1 = (bf16[160,384]{1,0:T(8,128)(2,1)S(1)}, bf16[160,384]{1,0:T(8,128)(2,1)S(1)}, u32[]{:S(2)}, u32[]{:S(2)}) collective-permute-start(bf16[160,384]{1,0:T(8,128)(2,1)S(1)} %get-tuple-element.26), channel_id=1, source_target_pairs={{16,32},{32,16},{48,64},{64,48},{80,96},{96,80},{17,33},{33,17},{4... | collective-permute-start | bytes 368648 | tf_op jit(solution)/shard_map/ppermute | solution.py:447
  16.0 2.4 %copy-start = (bf16[3584,768]{1,0:T(8,128)(2,1)}, bf16[3584,768]{1,0:T(8,128)(2,1)S(1)}, u32[]{:S(2)}) copy-start(bf16[3584,768]{1,0:T(8,128)(2,1)S(1)} %get-tuple-element.33.wg2) | copy-start | bytes 16515076
  19.4 6.7 %collective-permute-start.2 = (bf16[144,384]{1,0:T(8,128)(2,1)S(1)}, bf16[144,384]{1,0:T(8,128)(2,1)S(1)}, u32[]{:S(2)}, u32[]{:S(2)}) collective-permute-start(bf16[144,384]{1,0:T(8,128)(2,1)S(1)} %get-tuple-element.31), channel_id=1, source_target_pairs={{0,1},{1,0},{2,3},{3,2},{4,5},{5,4},{6,7},{7,6},{8,9},{9,8},{10,11... | collective-permute-start | bytes 331784 | tf_op jit(solution)/shard_map/ppermute | solution.py:447
  20.8 7.2 %collective-permute-start.3 = (bf16[144,384]{1,0:T(8,128)(2,1)S(1)}, bf16[144,384]{1,0:T(8,128)(2,1)S(1)}, u32[]{:S(2)}, u32[]{:S(2)}) collective-permute-start(bf16[144,384]{1,0:T(8,128)(2,1)S(1)} %get-tuple-element.32), channel_id=1, source_target_pairs={{1,2},{2,1},{3,4},{4,3},{5,6},{6,5},{7,8},{8,7},{9,10},{10,9},{11,... | collective-permute-start | bytes 331784 | tf_op jit(solution)/shard_map/ppermute | solution.py:447
where the time goes:
time: 51.2 us; the launch traced here: 51 us
  Pallas kernels  36 us (70%)
  starting transfers between devices  10.6 us (21%)
  local copies, waits for them, and re-layouts  2.42 us (5%)
  waiting for transfers between devices  1.87 us (4%)
    pallas_call x1, Pallas kernels, on_device(): call(main_kernel, [shape((2, 96, 256), F32)], [SMEM] + [VMEM] * 11, [pltp...  23 us
    ppermute x4, starting transfers between devices, swapped(): return lax.ppermute(value, axis, pairs)  10.6 us
    pallas_call x1, Pallas kernels, on_device(): call(coarse_weights_kernel, [shape((KC, 2 * C2), BF16), shape((KC, C2), B...  5.85 us
    pallas_call x1, Pallas kernels, on_device(): call(start_kernel, [shape((RC, CC, C2), BF16), shape((RF, CF, C1), BF16),...  3.75 us
    unnamed x2, local copies, waits for them, and re-layouts  2.42 us
    pallas_call x1, Pallas kernels, on_device(): call(fine_weights_kernel, [shape((18 * C1, 2 * C1), BF16), shape((C1, 18...  2.36 us
    ppermute x4, waiting for transfers between devices, swapped(): return lax.ppermute(value, axis, pairs)  1.87 us
  transfers between devices with their start and end apart: 4, of which 1 were waited for; matrix products, arithmetic and copies ran while one was open for 0% of the time, Pallas kernels for 16%

commit v1 on v0

v1 whole, which is shorter than its diff:
```python
import functools

import jax
import jax.numpy as jnp
from jax import lax
from jax.experimental import pallas as pl
from jax.experimental.pallas import tpu as pltpu
from jax.sharding import PartitionSpec as P

F32 = jnp.float32
BF16 = jnp.bfloat16

C2, C1 = 384, 192
GRID_ROWS, GRID_COLS = 48, 256
RC, CC = 6, 16
RF, CF = 12, 32
HC, HF = 5, 4
EC, EF = RC + 2 * HC, RF + 2 * HF
PC = 32
QC, QF = 24, 40
PAD = 8
WF = 256
ROW_BUF, COL_BUF = 160, 144
TAPS = 9
KC = TAPS * C2 + 128

VMEM = pl.BlockSpec(memory_space=pltpu.VMEM)
SMEM = pl.BlockSpec(memory_space=pltpu.SMEM)
ANY = pl.BlockSpec(memory_space=pl.ANY)
HBM = pl.BlockSpec(memory_space=pltpu.HBM)


def dot(a, b):
    return jnp.dot(a, b, preferred_element_type=F32)


def dot_t(a, b):
    return lax.dot_general(a, b, (((1,), (1,)), ((), ())), preferred_element_type=F32)


def sigmoid(x):
    return 0.5 * jnp.tanh(0.5 * x) + 0.5


def iota(shape, dim):
    return lax.broadcasted_iota(jnp.int32, shape, dim)


def tiles_get(ref, rows):
    return jnp.concatenate([ref[t, rows, :] for t in range(ref.shape[0])], 1)


def pack_pair(a, b):
    return jnp.concatenate([a[:, 128:], b[:, 128:], a[:, :128] + pltpu.roll(b[:, :128], 64, 1)], 1)


def unpack_pair(both):
    mixed = both[:, 256:384]
    upper = iota(mixed.shape, 1) >= 64
    a = jnp.where(upper, mixed, 0.0)
    b = jnp.where(upper, pltpu.roll(mixed, 64, 1), 0.0)
    return jnp.concatenate([a, both[:, :128]], 1), jnp.concatenate([b, both[:, 128:256]], 1)


def tiles_put(ref, rows, value):
    lanes = ref.shape[0] * 128
    if value.shape[1] < lanes:
        value = jnp.concatenate([value, jnp.zeros((value.shape[0], lanes - value.shape[1]), F32)], 1)
    for t in range(ref.shape[0]):
        ref[t, rows, :] = value[:, 128 * t : 128 * t + 128]


def indicator(cond):
    return jnp.where(cond, 1.0, 0.0).astype(BF16)


def start_kernel(
    place,
    frames_hbm,
    noise_hbm,
    context2_hbm,
    context1_hbm,
    hc_out,
    hf_out,
    noise_out,
    even_out,
    odd_out,
    frames,
    noise,
    context2,
    context1,
    picks,
    swaps,
    spreads,
    buf,
    sem,
):
    moves = [
        pltpu.make_async_copy(src, dst, sem.at[i])
        for i, (src, dst) in enumerate(
            (
                (frames_hbm, frames),
                (context2_hbm, context2),
                (context1_hbm, context1.at[pl.ds(WF - C1, C1), :]),
                (noise_hbm, noise),
            )
        )
    ]
    for copy in moves:
        copy.start()

    def pick(shift, parity):
        row, col = iota((128, 256), 0), iota((128, 256), 1)
        count = 256 >> shift
        j = 2 * (row >> (8 - shift)) + parity
        return indicator(col == ((row & (count - 1)) << shift) + j)

    context1[0 : WF - C1, :] = jnp.zeros((WF - C1, 256), BF16)
    for shift in (4, 3):
        for parity in range(2):
            picks[4 - shift, parity] = pick(shift, parity)
    row, col = iota((256, 256), 0), iota((256, 256), 1)
    swaps[...] = indicator(col == ((row & 15) << 4) + (row >> 4))
    row, col = iota((512, 256), 0), iota((512, 256), 1)
    source = (((row >> 4) & 3) << 6) + ((row & 7) << 3) + (row >> 6)
    for q in range(2):
        spreads[q] = indicator((col == source) & (((row >> 3) & 1) == q))
    moves[0].wait()
    zeros = jnp.zeros((64, 256), BF16)
    even, odd = [], []
    for r in range(RC):
        band = frames[:, 16 * r : 16 * r + 16, :].reshape(64, 256)
        even += [band, zeros]
        odd += [zeros, band]
    even, odd = jnp.concatenate(even, 0), jnp.concatenate(odd, 0)

    def turned(shift):
        both = dot_t(picks[4 - shift, 0], even) + dot_t(picks[4 - shift, 1], odd)
        return both.astype(BF16)

    deep = turned(4)
    left = jnp.concatenate(
        [
            jnp.concatenate([deep[16 * j : 16 * j + 16, 128 * r : 128 * r + 128] for r in range(RC)], 0)
            for j in range(8)
        ],
        1,
    )
    moves[1].wait()
    swap = swaps[...]
    moved = [dot(swap, context2[256 * f : 256 * f + 256, :]).astype(BF16) for f in range(4)]
    weight = jnp.concatenate([moved[f][16 * j : 16 * j + 16] for j in range(16) for f in range(4)], 0)
    state2 = jnp.tanh(dot(left, weight))
    hc_out[...] = state2.astype(BF16).reshape(RC, CC, C2)

    deep = turned(3)
    left = jnp.concatenate(
        [
            jnp.concatenate([deep[32 * j : 32 * j + 32, 128 * r : 128 * r + 128] for r in range(RC)], 0)
            for j in range(4)
        ],
        1,
    )
    moves[2].wait()
    for q in range(2):
        weight = dot_t(spreads[q], context1[...]).astype(BF16)
        state1 = jnp.tanh(dot(left, weight)).astype(BF16)
        for r in range(RC):
            hf_out[2 * r + q] = state1[CF * r : CF * r + CF]

    moves[3].wait()
    diagonal = indicator(iota((16, 16), 0) == iota((16, 16), 1))
    turned_noise = dot_t(diagonal, noise[...].reshape(RC * 8, CC))
    turned_noise = jnp.concatenate([turned_noise, jnp.zeros((16, 128 - 8 * RC), F32)], 1)
    noise_out[...] = turned_noise.astype(BF16)
    low_noise = pltpu.roll(turned_noise, 128 - 8 * (RC - HC), 1)

    up_first = (place[0] & 1) == 1
    for target, up in ((even_out, up_first), (odd_out, jnp.logical_not(up_first))):
        c_top = state2[: HC * CC]
        c_low = state2[(RC - HC) * CC :]
        buf[0:80, :] = jnp.where(up, c_top, c_low)
        top = [hf_out[r : r + 2].reshape(64, WF).astype(F32) for r in (0, 2)]
        low = [hf_out[r : r + 2].reshape(64, WF).astype(F32) for r in (RF - HF, RF - HF + 2)]
        buf[80:144, :] = jnp.where(up, pack_pair(*top), pack_pair(*low))
        buf[144:160, :] = jnp.zeros((16, C2), F32)
        buf[144:160, 0:128] = jnp.where(up, turned_noise, low_noise)
        target[...] = buf[...].astype(BF16)


def column_kernel(
    place, hc, hf, noise, even_in, odd_in, after, ec_out, ef_out, en_out, even_out, odd_out, sc, sf, sn, buf
):
    up_first = (place[0] & 1) == 1
    above = jnp.where(up_first, even_in[...].astype(F32), odd_in[...].astype(F32))
    below = jnp.where(up_first, odd_in[...].astype(F32), even_in[...].astype(F32))
    tiles_put(sc, pl.ds(0, 80), above[0:80])
    tiles_put(sc, pl.ds(80, 96), hc[...].reshape(RC * CC, C2).astype(F32))
    tiles_put(sc, pl.ds(176, 80), below[0:80])
    for half, strip in enumerate(unpack_pair(above[80:144])):
        tiles_put(sf, pl.ds(64 * half, 64), strip)
    for half, strip in enumerate(unpack_pair(below[80:144])):
        tiles_put(sf, pl.ds(512 + 64 * half, 64), strip)
    tiles_put(sf, pl.ds(128, 384), hf[...].reshape(RF * CF, WF).astype(F32))
    tiles_put(sf, pl.ds(640, 128), jnp.zeros((128, WF), F32))
    sn[...] = jnp.zeros(sn.shape, F32)
    for h in range(HC):
        sn[16 * h : 16 * h + 16, 0:8] = above[144:160, 8 * h : 8 * h + 8]
        sn[16 * (HC + RC + h) : 16 * (HC + RC + h) + 16, 0:8] = below[144:160, 8 * h : 8 * h + 8]
    for h in range(RC):
        sn[16 * (HC + h) : 16 * (HC + h) + 16, 0:8] = noise[:, 8 * h : 8 * h + 8].astype(F32)

    ec_out[...] = tiles_get(sc, pl.ds(0, EC * CC)).astype(BF16).reshape(EC, CC, C2)
    ef_out[...] = tiles_get(sf, pl.ds(0, EF * CF)).astype(BF16).reshape(EF, CF, WF)
    en_out[...] = sn[...].astype(BF16).reshape(EC, CC, 128)

    left_first = (place[1] & 1) == 1
    for target, left in ((even_out, left_first), (odd_out, jnp.logical_not(left_first))):
        c_from = jnp.where(left, 0, CC - HC)
        f_from = jnp.where(left, 0, CF - HF)
        buf[128:144, :] = jnp.zeros((16, C2), F32)
        for k in range(HC):
            buf[16 * k : 16 * k + 16, :] = tiles_get(sc, pl.ds(c_from + k, 16, stride=CC))
            strip = sn[pl.ds(c_from + k, 16, stride=CC), :]
            buf[128:144, 8 * k : 8 * k + 8] = strip[:, 0:8]
        for k in range(2):
            strips = [tiles_get(sf, pl.ds(f_from + i, 24, stride=CF)) for i in (k, k + 2)]
            buf[80 + 24 * k : 104 + 24 * k, :] = pack_pair(*strips)
        target[...] = buf[...].astype(BF16)


def coarse_weights_kernel(
    proj_hbm, gates_hbm, cand_hbm, wg_out, wc_out, token, proj, gates, cand, acc_g, acc_c, sem
):
    count = [0]

    def move(src, dst):
        copy = pltpu.make_async_copy(src, dst, sem.at[count[0]])
        count[0] += 1
        copy.start()
        return copy

    first = move(proj_hbm, proj)
    inputs, states = [], []
    for hbm, held in ((gates_hbm, gates), (cand_hbm, cand)):
        inputs.append([move(hbm.at[pl.ds(2 * C2 * t, C2), :], held.at[t]) for t in range(TAPS)])
    for hbm, target in ((gates_hbm, wg_out), (cand_hbm, wc_out)):
        for t in range(TAPS):
            states.append(move(hbm.at[pl.ds(2 * C2 * t + C2, C2), :], target.at[pl.ds(C2 * t, C2), :]))
    acc_g[...] = jnp.zeros(acc_g.shape, F32)
    acc_c[...] = jnp.zeros(acc_c.shape, F32)
    first.wait()
    token[...] = jnp.zeros(token.shape, F32)
    wide = jnp.concatenate([proj[...].astype(F32), jnp.zeros((8, C2), F32)], 0).astype(BF16)
    for copies, held, acc in ((inputs[0], gates, acc_g), (inputs[1], cand, acc_c)):
        for t in range(TAPS):
            copies[t].wait()
            acc[8 * t : 8 * t + 8, :] = dot(wide, held[t])[0:8]
    wg_out[TAPS * C2 :, :] = acc_g[...].astype(BF16)
    wc_out[TAPS * C2 :, :] = acc_c[...].astype(BF16)
    for copy in states:
        copy.wait()


def fine_weights_kernel(
    after, gates_hbm, cand_hbm, up_hbm, head_hbm, wr_out, wu_out, wv_out, wc_out, up_out, head_out, gates, up, head, sem
):
    moves = [
        pltpu.make_async_copy(src, dst, sem.at[i])
        for i, (src, dst) in enumerate(
            (
                (up_hbm, up),
                (head_hbm, head),
                (gates_hbm, gates),
                (cand_hbm, wc_out.at[pl.ds(WF - C1, C1), :]),
            )
        )
    ]
    for copy in moves:
        copy.start()
    wc_out[0 : WF - C1, :] = jnp.zeros((WF - C1, 18 * C1), BF16)
    moves[1].wait()
    row, col = iota((1024, 64), 0), iota((1024, 64), 1)
    spread = indicator(col == ((row >> 7) << 3) + (row & 7))
    wide = jnp.concatenate([jnp.zeros((64, WF - C1), F32), head[...].astype(F32)], 1).astype(BF16)
    head_out[...] = dot(spread, wide).astype(BF16)
    moves[0].wait()
    wide = up[...].astype(F32)
    zeros = jnp.zeros((C2, 256 - C1), F32)
    for i in range(4):
        part = jnp.concatenate([wide[:, C1 * i : C1 * i + C1], zeros], 1)
        up_out[:, 256 * i : 256 * i + 256] = part.astype(BF16)
    moves[2].wait()
    for t in range(TAPS):
        rows = slice(2 * C1 * t, 2 * C1 * t + 2 * C1)
        part = gates[rows, 0:256].astype(F32)
        wr_out[rows, :] = jnp.concatenate([part[:, C1:256], part[:, :C1]], 1).astype(BF16)
        target, lane = (wv_out, 0) if t % 3 == 1 else (wu_out, 64 * (t % 3))
        target[2 * C1 * (t // 3) : 2 * C1 * (t // 3) + 2 * C1, lane : lane + 128] = gates[rows, 256:384]
    moves[3].wait()


def main_kernel(
    place,
    ec,
    ef,
    en,
    even_in,
    odd_in,
    wg2,
    wc2,
    wr1,
    wu1,
    wv1,
    wc1,
    wup,
    whead,
    out,
    first_h,
    sn,
    patch,
    reset_h,
    next_h,
    gate_u,
    fine_x,
    fine_h,
    fine_reset,
    fine_u,
    side_u,
    even_c,
    odd_c,
    even_f,
    odd_f,
    last_f,
):
    row0, col0 = place[0], place[1]
    left_first = (col0 & 1) == 1
    left = jnp.where(left_first, even_in[...].astype(F32), odd_in[...].astype(F32))
    right = jnp.where(left_first, odd_in[...].astype(F32), even_in[...].astype(F32))

    for ref, pitch, rows in (
        (reset_h, QC, EC), (next_h, QC, EC), (fine_x, QF, EF), (fine_h, QF, EF), (fine_reset, QF, EF)
    ):
        for t in range(ref.shape[0]):
            ref[t, 0 : PAD + 2 * pitch, :] = jnp.zeros((PAD + 2 * pitch, 128), F32)
            ref[t, PAD + (rows - 2) * pitch :, :] = jnp.zeros((2 * pitch + 8, 128), F32)
    sn[...] = jnp.zeros(sn.shape, F32)
    for h in range(EC):
        tiles_put(first_h, pl.ds(PC * h + 8, CC), ec[h].astype(F32))
        sn[PC * h + 8 : PC * h + 24, :] = en[h].astype(F32)
    for k in range(HC):
        for side, at in ((left, 8 - HC + k), (right, 8 + CC + k)):
            tiles_put(first_h, pl.ds(at, EC, stride=PC), side[16 * k : 16 * k + 16])
            strip = jnp.concatenate([side[128:144, 8 * k : 8 * k + 8], jnp.zeros((16, 120), F32)], 1)
            sn[pl.ds(at, EC, stride=PC), :] = strip
    for h in range(EF):
        tiles_put(fine_h, pl.ds(PAD + QF * h + HF, CF), ef[h].astype(F32))
    for side, col in ((left, 0), (right, HF + CF)):
        for k in range(2):
            for i, strip in enumerate(unpack_pair(side[80 + 24 * k : 80 + 24 * k + EF])):
                tiles_put(fine_h, pl.ds(PAD + col + k + 2 * i, EF, stride=QF), strip)

    noise = sn[...].reshape(EC, PC, 128)
    total = None
    for dx in range(3):
        part = None
        for dy in range(3):
            moved = noise[dy : dy + EC - 2]
            if dy or dx:
                moved = pltpu.roll(moved, 8 * (3 * dy + dx), 2)
            part = moved if part is None else part + moved
        part = part[:, 3 + dx : 3 + dx + QC, :]
        total = part if total is None else total + part
    patch[...] = total.reshape((EC - 2) * QC, 128)

    def fill(even, odd, pitch, lane, first, last, window):
        for dx in range(3):
            for ref, start in ((even, first + first % 2), (odd, first + 1 - first % 2)):
                rows = last - first - 2 * (start != first)
                at = (start // 2) * 2 * pitch
                ref[dx, at : at + rows * pitch, lane : lane + 128] = window(start, rows, dx - 1).astype(BF16)

    def taps(even, odd, pitch, first, rows):
        parts = []
        for dy in range(3):
            start = first - 1 + dy
            ref = odd if start % 2 else even
            at = (start // 2) * 2 * pitch
            parts += [ref[dx, at : at + rows * pitch, :] for dx in range(3)]
        return parts

    def flat(ref, t, pitch):
        return lambda start, rows, shift: ref[t, pl.ds(PAD + start * pitch + shift, rows * pitch), :]

    def cells(ref, t, pitch, first, rows):
        return ref[t, pl.ds(PAD + first * pitch, rows * pitch), :]

    def valid(first, rows, pitch, row_own, col_own, scale):
        at = iota((rows, pitch, 128), 0) + (row_own * scale + first)
        col = iota((rows, pitch, 128), 1) + (col_own * scale)
        good = (at >= 0) & (at < GRID_ROWS * scale) & (col >= 0) & (col < GRID_COLS * scale)
        return good.reshape(rows * pitch, 128)

    def own_first(t, start, rows, shift):
        return jnp.concatenate(
            [first_h[t, pl.ds(PC * h + 4 + shift, QC), :] for h in range(start, start + rows)], 0
        )

    def coarse_left(first, rows):
        near = patch[QC * (first - 1) : QC * (first - 1 + rows), :].astype(BF16)
        return jnp.concatenate(taps(even_c, odd_c, QC, first, rows) + [near], 1)

    def coarse_gates(step):
        first, rows = 1 + 2 * step, 14 - 4 * step
        for t in range(3):
            if step == 0:
                window = functools.partial(own_first, t)
            else:
                window = flat(next_h, t, QC)
            fill(even_c, odd_c, QC, 128 * t, first - 1, first + rows + 1, window)
        operand = coarse_left(first, rows)
        gates = dot(operand, wg2[:, 0:512])
        for t in range(3):
            old = own_first(t, first, rows, 0) if step == 0 else cells(next_h, t, QC, first, rows)
            reset_h[t, pl.ds(PAD + QC * first, QC * rows), :] = sigmoid(gates[:, 128 * t : 128 * t + 128]) * old
        gate_u[0, pl.ds(PAD + QC * first, QC * rows), :] = sigmoid(gates[:, 384:512])
        gates = dot(coarse_left(first + 1, rows - 2), wg2[:, 512:768])
        for t in (1, 2):
            at = pl.ds(PAD + QC * (first + 1), QC * (rows - 2))
            gate_u[t, at, :] = sigmoid(gates[:, 128 * t - 128 : 128 * t])

    def coarse_cand(step):
        first, rows = 2 + 2 * step, 12 - 4 * step
        for t in range(3):
            fill(even_c, odd_c, QC, 128 * t, first - 1, first + rows + 1, flat(reset_h, t, QC))
        operand = coarse_left(first, rows)
        good = valid(first, rows, QC, row0 * RC - HC, col0 * CC - 4, 1)
        for lanes, here in ((slice(0, 256), (0, 1)), (slice(256, 384), (2,))):
            cand = jnp.tanh(dot(operand, wc2[:, lanes]))
            for i, t in enumerate(here):
                new = cand[:, 128 * i : 128 * i + 128]
                old = own_first(t, first, rows, 0) if step == 0 else cells(next_h, t, QC, first, rows)
                new = new + cells(gate_u, t, QC, first, rows) * (old - new)
                new = jnp.where(good, new, 0.0).astype(BF16).astype(F32)
                next_h[t, pl.ds(PAD + QC * first, QC * rows), :] = new

    def fine_input(step):
        first, rows = 3 + step, 10 - 2 * step
        state = jnp.concatenate(
            [
                jnp.concatenate(
                    [next_h[t, pl.ds(PAD + QC * h + 2, QC), :] for h in range(first, first + rows)], 0
                )
                for t in range(3)
            ],
            1,
        ).astype(BF16)
        value = dot(state, wup[...])
        for q in range(2):
            for p in range(2):
                lane = 256 * (2 * q + p)
                for r in range(rows):
                    at = PAD + (2 * (first + r) - 6 + q) * QF + p
                    tiles_put(fine_x, pl.ds(at, 20, stride=2), value[QC * r : QC * r + 20, lane : lane + 256])

    def fine_mixed(state, first, last):
        fill(even_f, odd_f, QF, 128, first, last, lambda *w: flat(fine_x, 1, QF)(*w) + flat(state, 0, QF)(*w))

    def fine_before(step):
        first, rows = 1 + 2 * step, 18 - 4 * step
        fill(even_f, odd_f, QF, 256, first - 1, first + rows + 1, flat(fine_h, 1, QF))

    def fine_gates(step):
        first, rows = 1 + 2 * step, 18 - 4 * step
        fill(even_f, odd_f, QF, 0, first - 1, first + rows + 1, flat(fine_x, 0, QF))
        fine_mixed(fine_h, first - 1, first + rows + 1)
        gates = dot(jnp.concatenate(taps(even_f, odd_f, QF, first, rows), 1), wr1[...])
        at = pl.ds(PAD + QF * first, QF * rows)
        gate = sigmoid(gates[:, 0:128])
        fine_reset[0, at, :] = gate * fine_h[0, at, :]
        fine_u[0, at, :] = pltpu.roll(gate, 64, 1)
        fine_reset[1, at, :] = sigmoid(gates[:, 128:256]) * fine_h[1, at, :]
        middle = jnp.concatenate(taps(even_f, odd_f, QF, first + 1, rows - 2)[1::3], 1)
        count = QF * (rows - 2)
        sides = dot(middle, wu1[...])
        for i in range(2):
            side_u[i, PAD : PAD + count, :] = sides[:, 128 * i : 128 * i + 128]
        gate = dot(middle, wv1[...]) + side_u[0, pl.ds(PAD - 1, count), :] + side_u[1, pl.ds(PAD + 1, count), :]
        fine_u[1, pl.ds(PAD + QF * (first + 1), count), :] = sigmoid(gate)

    def fine_cand():
        first, rows = 2, 16
        fine_mixed(fine_reset, first - 1, first + rows + 1)
        fill(even_f, odd_f, QF, 256, first - 1, first + rows + 1, flat(fine_reset, 1, QF))
        operand = jnp.concatenate(taps(even_f, odd_f, QF, first, rows), 1)
        good = valid(first, rows, QF, row0 * RC - HC + 3, col0 * CC - 2, 2)
        cand = jnp.tanh(dot_t(operand, wc1[...]))
        at = pl.ds(PAD + QF * first, QF * rows)
        for t in range(2):
            new = cand[:, 128 * t : 128 * t + 128]
            new = new + fine_u[t, at, :] * (fine_h[t, at, :] - new)
            fine_h[t, at, :] = jnp.where(good, new, 0.0).astype(BF16).astype(F32)

    def own_fine(ref, t, shift=0, first=HF, rows=RF):
        return jnp.concatenate(
            [ref[t, pl.ds(PAD + QF * h + HF + shift, CF), :] for h in range(first, first + rows)], 0
        )

    def fine_last():
        first, rows = HF - 1, RF + 2
        for dx in range(3):
            x1 = own_fine(fine_x, 1, dx - 1, first, rows) + own_fine(fine_reset, 0, dx - 1, first, rows)
            last_f[dx, :, 0:128] = own_fine(fine_x, 0, dx - 1, first, rows).astype(BF16)
            last_f[dx, :, 128:256] = x1.astype(BF16)
            last_f[dx, :, 256:384] = own_fine(fine_reset, 1, dx - 1, first, rows).astype(BF16)
        parts = [last_f[dx, CF * dy : CF * (dy + RF), :] for dy in range(3) for dx in range(3)]
        cand = jnp.tanh(dot_t(jnp.concatenate(parts, 1), wc1[...]))
        state = []
        for t in range(2):
            new = cand[:, 128 * t : 128 * t + 128]
            state.append(new + own_fine(fine_u, t) * (own_fine(fine_h, t) - new))
        return jnp.concatenate(state, 1).astype(BF16)

    def emit(step, state):
        rows = RF
        shape = (2 * rows, 8, 128)
        lane, cell = iota(shape, 2), iota(shape, 1)
        low, mine = lane < 64, ((lane >> 3) & 7) == cell
        lines = []
        for r in range(0, 8, 2):
            pair = dot_t(state, whead[128 * r : 128 * r + 256, :])
            for i in range(2):
                value = pair[:, 128 * i : 128 * i + 128].reshape(2 * rows, 2, 8, 128)
                lines.append(jnp.where(mine, jnp.where(low, value[:, 0], value[:, 1]), 0.0))
        for d in (1, 2, 4):
            here = (cell & d) == 0
            folded = []
            for i in range(0, len(lines), 2):
                a, b = lines[i], lines[i + 1]
                folded.append(jnp.where(here, a, b) + pltpu.roll(jnp.where(here, b, a), d, 1))
            lines = folded
        final = lines[0].reshape(rows, 2, 8, 128)
        for t in range(2):
            out[step, :, 128 * t : 128 * t + 128] = final[:, t].reshape(8 * rows, 128)

    coarse_gates(0)
    fine_before(0)
    coarse_cand(0)
    fine_input(0)
    coarse_gates(1)
    fine_gates(0)
    coarse_cand(1)
    fine_cand()
    fine_input(1)
    emit(0, jnp.concatenate([own_fine(fine_h, 0), own_fine(fine_h, 1)], 1).astype(BF16))
    fine_before(1)
    fine_gates(1)
    emit(1, fine_last())


def in_hbm(value):
    return pltpu.with_memory_space_constraint(value, pltpu.HBM)


def swapped(value, axis, odd):
    pairs = []
    for i in range(odd, lax.axis_size(axis) - 1, 2):
        pairs += [(i, i + 1), (i + 1, i)]
    return lax.ppermute(value, axis, pairs)


def call(kernel, out_shape, in_specs, scratch, limit, flops, bytes_accessed, **extra):
    return pl.pallas_call(
        kernel,
        out_shape=out_shape,
        in_specs=in_specs,
        out_specs=[VMEM] * len(out_shape),
        scratch_shapes=scratch,
        compiler_params=pltpu.CompilerParams(vmem_limit_bytes=limit),
        cost_estimate=pl.CostEstimate(flops=flops, bytes_accessed=bytes_accessed, transcendentals=0),
        **extra,
    )


def on_device(
    context_frames,
    latent_noise,
    latent_proj,
    coarse_context,
    fine_context,
    coarse_gates,
    coarse_candidate,
    fine_gates,
    fine_candidate,
    upsample_proj,
    head_proj,
):
    place = jnp.stack([lax.axis_index("row"), lax.axis_index("col")]).astype(jnp.int32)
    shape = jax.ShapeDtypeStruct
    row_buf, col_buf = shape((ROW_BUF, C2), BF16), shape((COL_BUF, C2), BF16)

    hc, hf, noise, even, odd = call(
        start_kernel,
        [
            shape((RC, CC, C2), BF16),
            shape((RF, CF, WF), BF16),
            shape((16, 128), BF16),
            row_buf,
            row_buf,
        ],
        [SMEM] + [HBM] * 4,
        [
            pltpu.VMEM((4, 16 * RC, 16 * CC), BF16),
            pltpu.VMEM((RC, 8, CC), BF16),
            pltpu.VMEM((1024, C2), BF16),
            pltpu.VMEM((WF, 256), BF16),
            pltpu.VMEM((2, 2, 128, 256), BF16),
            pltpu.VMEM((256, 256), BF16),
            pltpu.VMEM((2, 512, 256), BF16),
            pltpu.VMEM((ROW_BUF, C2), F32),
            pltpu.SemaphoreType.DMA((4,)),
        ],
        16 << 20, 10**9, 2 << 20,
    )(
        place,
        in_hbm(context_frames),
        in_hbm(latent_noise.transpose(0, 2, 1)),
        in_hbm(coarse_context),
        in_hbm(fine_context.T),
    )

    even, odd = swapped(even, "row", 0), swapped(odd, "row", 1)

    wg2, wc2, token = call(
        coarse_weights_kernel,
        [shape((KC, 2 * C2), BF16), shape((KC, C2), BF16), shape((8, 128), F32)],
        [HBM] * 3,
        [
            pltpu.VMEM((8, C2), BF16),
            pltpu.VMEM((TAPS, C2, 2 * C2), BF16),
            pltpu.VMEM((TAPS, C2, C2), BF16),
            pltpu.VMEM((128, 2 * C2), F32),
            pltpu.VMEM((128, C2), F32),
            pltpu.SemaphoreType.DMA((4 * TAPS + 1,)),
        ],
        16 << 20, 10**9, 24 << 20,
    )(in_hbm(latent_proj), in_hbm(coarse_gates), in_hbm(coarse_candidate))

    ec, ef, en, even, odd = call(
        column_kernel,
        [
            shape((EC, CC, C2), BF16),
            shape((EF, CF, WF), BF16),
            shape((EC, CC, 128), BF16),
            col_buf,
            col_buf,
        ],
        [SMEM] + [VMEM] * 5 + [ANY],
        [
            pltpu.VMEM((3, EC * CC, 128), F32),
            pltpu.VMEM((2, 24 * CF, 128), F32),
            pltpu.VMEM((EC * CC, 128), F32),
            pltpu.VMEM((COL_BUF, C2), F32),
        ],
        8 << 20, 10**6, 2 << 20,
    )(place, hc, hf, noise, even, odd, token)

    even, odd = swapped(even, "col", 0), swapped(odd, "col", 1)

    wr1, wu1, wv1, wc1, up, head = call(
        fine_weights_kernel,
        [
            shape((18 * C1, 256), BF16),
            shape((6 * C1, 256), BF16),
            shape((6 * C1, 128), BF16),
            shape((WF, 18 * C1), BF16),
            shape((C2, 1024), BF16),
            shape((1024, WF), BF16),
        ],
        [ANY] + [HBM] * 4,
        [
            pltpu.VMEM((18 * C1, 2 * C1), BF16),
            pltpu.VMEM((C2, 4 * C1), BF16),
            pltpu.VMEM((64, C1), BF16),
            pltpu.SemaphoreType.DMA((4,)),
        ],
        12 << 20, 10**8, 8 << 20,
    )(en, in_hbm(fine_gates), in_hbm(fine_candidate.T), in_hbm(upsample_proj), in_hbm(head_proj.T))

    (forecast,) = call(
        main_kernel,
        [shape((2, 96, 256), F32)],
        [SMEM] + [VMEM] * 13,
        [
            pltpu.VMEM((3, EC * PC, 128), F32),
            pltpu.VMEM((EC * PC, 128), F32),
            pltpu.VMEM(((EC - 2) * QC, 128), F32),
            pltpu.VMEM((3, PAD + EC * QC + 8, 128), F32),
            pltpu.VMEM((3, PAD + EC * QC + 8, 128), F32),
            pltpu.VMEM((3, PAD + EC * QC + 8, 128), F32),
            pltpu.VMEM((2, PAD + EF * QF + 8, 128), F32),
            pltpu.VMEM((2, PAD + EF * QF + 8, 128), F32),
            pltpu.VMEM((2, PAD + EF * QF + 8, 128), F32),
            pltpu.VMEM((2, PAD + EF * QF + 8, 128), F32),
            pltpu.VMEM((2, PAD + 16 * QF + 8, 128), F32),
            pltpu.VMEM((3, EC * QC, C2), BF16),
            pltpu.VMEM((3, EC * QC, C2), BF16),
            pltpu.VMEM((3, EF * QF, 2 * C1), BF16),
            pltpu.VMEM((3, EF * QF, 2 * C1), BF16),
            pltpu.VMEM((3, (RF + 2) * CF, 2 * C1), BF16),
        ],
        26 << 20, 9 * 10**9, 30 << 20,
    )(place, ec, ef, en, even, odd, wg2, wc2, wr1, wu1, wv1, wc1, up, head)
    return forecast


def solution(mesh):
    return jax.shard_map(
        on_device,
        mesh=mesh,
        in_specs=(
            P(None, "row", "col"),
            P("row", "col", None),
            P(),
            P(),
            P(),
            P(),
            P(),
            P(),
            P(),
            P(),
            P(),
        ),
        out_specs=P(None, "row", "col"),
        check_vma=False,
    )
```

time: 51.2 us -> 41.9 us (0.82)
  Pallas kernels: 36 us -> 29.5 us
  local copies, waits for them, and re-layouts: 2.42 us -> 0 us
    pallas_call x4, Pallas kernels: 30.1 us -> 23.7 us  [the longest x1 16.2 us: on_device(): call(main_kernel, [shape((2, 96, 256), F32)], [SMEM] + [VMEM] * 13, [pltp...]
    unnamed x2 -> x0, local copies, waits for them, and re-layouts: 2.42 us -> none
  transfers between devices with their start and end apart: 4 -> 4, of which waited for: 1 -> 1; matrix products, arithmetic and copies ran while one was open for 0% -> 0% of each run, Pallas kernels for 16% -> 21%
where the time goes in v1:
time: 41.9 us; the launch traced here: 41.7 us
  Pallas kernels  29.5 us (70%)
  starting transfers between devices  10.6 us (25%)
  waiting for transfers between devices  1.46 us (3%)
    pallas_call x1, Pallas kernels, on_device(): call(main_kernel, [shape((2, 96, 256), F32)], [SMEM] + [VMEM] * 13, [pltp...  16.2 us
    ppermute x4, starting transfers between devices, swapped(): return lax.ppermute(value, axis, pairs)  10.6 us
    pallas_call x1, Pallas kernels, on_device(): call(coarse_weights_kernel, [shape((KC, 2 * C2), BF16), shape((KC, C2), B...  5.85 us
    pallas_call x1, Pallas kernels, on_device(): call(start_kernel, [shape((RC, CC, C2), BF16), shape((RF, CF, WF), BF16),...  3.71 us
    pallas_call x1, Pallas kernels, on_device(): call(fine_weights_kernel, [shape((18 * C1, 256), BF16), shape((6 * C1, 25...  2.77 us
    ppermute x4, waiting for transfers between devices, swapped(): return lax.ppermute(value, axis, pairs)  1.46 us
    pallas_call x1, Pallas kernels, on_device(): call(column_kernel, [shape((EC, CC, C2), BF16), shape((EF, CF, WF), BF16)...  0.97 us
  transfers between devices with their start and end apart: 4, of which 1 were waited for; matrix products, arithmetic and copies ran while one was open for 0% of the time, Pallas kernels for 21%

profile of v1, /device:TPU:19, one launch (start us, length us, event | category | flops | bytes accessed | tf_op | source)
XLA Modules:
  0.0 41.7 jit_solution(13510857988122035014)
XLA Ops:
  0.0 0.1 pad_add_fusion.place
  0.1 3.7 %shard_map.109 = (bf16[6,16,384]{2,1,0:T(8,128)(2,1)S(1)}, bf16[12,32,256]{2,1,0:T(8,128)(2,1)S(1)}, bf16[16,128]{1,0:T(8,128)(2,1)S(1)}, bf16[160,384]{1,0:T(8,128)(2,1)S(1)}, bf16[160,384]{1,0:T(8,128)(2,1)S(1)}) custom-call(s32[2]{0:T(128)S(1)} %pad_add_fusion.place, bf16[4,96,256]{2,1,0:T(8,128)(2,1)} %frames_hbm.1, bf16[6,8,16]{2,1,0:T(8,128)(2,1)} %bitcast.9, ...), custom_call_target="tpu_custom_call" | custom-call | flops 1000000000 | bytes 2097152 | tf_op jit(solution)/shard_map/pallas_call | solution.py:602
  3.8 0.1 collective-permute-start
  3.9 6.2 %collective-permute-start.1 = (bf16[160,384]{1,0:T(8,128)(2,1)S(1)}, bf16[160,384]{1,0:T(8,128)(2,1)S(1)}, u32[]{:S(2)}, u32[]{:S(2)}) collective-permute-start(bf16[160,384]{1,0:T(8,128)(2,1)S(1)} %get-tuple-element.28), channel_id=1, source_target_pairs={{16,32},{32,16},{48,64},{64,48},{80,96},{96,80},{17,33},{33,17},{4... | collective-permute-start | bytes 368648 | tf_op jit(solution)/shard_map/ppermute | solution.py:569
  10.1 5.8 %shard_map.110 = (bf16[3584,768]{1,0:T(8,128)(2,1)S(1)}, bf16[3584,384]{1,0:T(8,128)(2,1)S(1)}, f32[8,128]{1,0:T(8,128)S(1)}) custom-call(bf16[8,384]{1,0:T(8,128)(2,1)} %proj_hbm.1, bf16[6912,768]{1,0:T(8,128)(2,1)} %gates_hbm.2, bf16[6912,384]{1,0:T(8,128)(2,1)} %cand_hbm.1), custom_call_target="tpu_custom_call" | custom-call | flops 1000000000 | bytes 25165824 | tf_op jit(solution)/shard_map/pallas_call | solution.py:634
  16.0 0.0 collective-permute-done.even_in
  16.0 0.0 collective-permute-done.1.odd_in
  16.0 1.0 %shard_map.111 = (bf16[16,16,384]{2,1,0:T(8,128)(2,1)S(1)}, bf16[20,32,256]{2,1,0:T(8,128)(2,1)S(1)}, bf16[16,16,128]{2,1,0:T(8,128)(2,1)S(1)}, bf16[144,384]{1,0:T(8,128)(2,1)S(1)}, bf16[144,384]{1,0:T(8,128)(2,1)S(1)}) custom-call(s32[2]{0:T(128)S(1)} %pad_add_fusion.place, bf16[6,16,384]{2,1,0:T(8,128)(2,1)S(1)} %get-tuple-element.24.hc, ...), custom_call_target="tpu_custom_call" | custom-call | flops 1000000 | bytes 2097152 | tf_op jit(solution)/shard_map/pallas_call | solution.py:649
  16.9 1.3 %collective-permute-start.2 = (bf16[144,384]{1,0:T(8,128)(2,1)S(1)}, bf16[144,384]{1,0:T(8,128)(2,1)S(1)}, u32[]{:S(2)}, u32[]{:S(2)}) collective-permute-start(bf16[144,384]{1,0:T(8,128)(2,1)S(1)} %get-tuple-element.33), channel_id=1, source_target_pairs={{0,1},{1,0},{2,3},{3,2},{4,5},{5,4},{6,7},{7,6},{8,9},{9,8},{10,11... | collective-permute-start | bytes 331784 | tf_op jit(solution)/shard_map/ppermute | solution.py:569
  18.3 3.0 %collective-permute-start.3 = (bf16[144,384]{1,0:T(8,128)(2,1)S(1)}, bf16[144,384]{1,0:T(8,128)(2,1)S(1)}, u32[]{:S(2)}, u32[]{:S(2)}) collective-permute-start(bf16[144,384]{1,0:T(8,128)(2,1)S(1)} %get-tuple-element.34), channel_id=1, source_target_pairs={{1,2},{2,1},{3,4},{4,3},{5,6},{6,5},{7,8},{8,7},{9,10},{10,9},{11,... | collective-permute-start | bytes 331784 | tf_op jit(solution)/shard_map/ppermute | solution.py:569
  21.3 2.8 %shard_map.112 = (bf16[3456,256]{1,0:T(8,128)(2,1)S(1)}, bf16[1152,256]{1,0:T(8,128)(2,1)S(1)}, bf16[1152,128]{1,0:T(8,128)(2,1)S(1)}, bf16[256,3456]{1,0:T(8,12...) custom-call(bf16[16,16,128]{2,1,0:T(8,128)(2,1)S(1)} %get-tuple-element.32.after.en, ...), custom_call_target="tpu_custom_call" | custom-call | flops 100000000 | bytes 8388608 | tf_op jit(solution)/shard_map/pallas_call | solution.py:670
  24.0 0.0 collective-permute-done.2.even_in
  24.1 1.5 %collective-permute-done.3.odd_in = bf16[144,384]{1,0:T(8,128)(2,1)S(1)} collective-permute-done((bf16[144,384]{1,0:T(8,128)(2,1)S(1)}, bf16[144,384]{1,0:T(8,128)(2,1)S(1)}, u32[]{:S(2)}, u32[]{:S(2)}) %collective-permute-start.3) | collective-permute-done | bytes 110624 | tf_op jit(solution)/shard_map/ppermute | solution.py:569
  25.5 16.2 %shard_map.113 = f32[2,96,256]{2,1,0:T(8,128)} custom-call(s32[2]{0:T(128)S(1)} %pad_add_fusion.place, bf16[16,16,384]{2,1,0:T(8,128)(2,1)S(1)} %get-tuple-element.30.ec, bf16[20,32,256]{2,1,0:T(8,128)(2,1)S(1)} %get-tuple-element.31.ef, bf16[16,16,128]{2,1,0:T(8,128)(2,1)S(1)} %get-tuple-element.32.after.en, ...), custom_call_target="tpu_custom_call" | custom-call | flops 8999999488 | bytes 31457280 | tf_op jit(solution)/shard_map/pallas_call | solution.py:690
Async XLA Ops:
  3.8 12.2 %collective-permute-start = (bf16[160,384]{1,0:T(8,128)(2,1)S(1)}, bf16[160,384]{1,0:T(8,128)(2,1)S(1)}, u32[]{:S(2)}, u32[]{:S(2)}) collective-permute-start(bf16[160,384]{1,0:T(8,128)(2,1)S(1)} %get-tuple-element.27), channel_id=1, source_target_pairs={{0,16},{16,0},{32,48},{48,32},{64,80},{80,64},{96,112},{112,96},{1... | collective-permute-start | bytes 368648 | tf_op jit(solution)/shard_map/ppermute | solution.py:569
  3.9 12.0 %collective-permute-start.1 = (bf16[160,384]{1,0:T(8,128)(2,1)S(1)}, bf16[160,384]{1,0:T(8,128)(2,1)S(1)}, u32[]{:S(2)}, u32[]{:S(2)}) collective-permute-start(bf16[160,384]{1,0:T(8,128)(2,1)S(1)} %get-tuple-element.28), channel_id=1, source_target_pairs={{16,32},{32,16},{48,64},{64,48},{80,96},{96,80},{17,33},{33,17},{4... | collective-permute-start | bytes 368648 | tf_op jit(solution)/shard_map/ppermute | solution.py:569
  16.9 7.1 %collective-permute-start.2 = (bf16[144,384]{1,0:T(8,128)(2,1)S(1)}, bf16[144,384]{1,0:T(8,128)(2,1)S(1)}, u32[]{:S(2)}, u32[]{:S(2)}) collective-permute-start(bf16[144,384]{1,0:T(8,128)(2,1)S(1)} %get-tuple-element.33), channel_id=1, source_target_pairs={{0,1},{1,0},{2,3},{3,2},{4,5},{5,4},{6,7},{7,6},{8,9},{9,8},{10,11... | collective-permute-start | bytes 331784 | tf_op jit(solution)/shard_map/ppermute | solution.py:569
  18.3 7.2 %collective-permute-start.3 = (bf16[144,384]{1,0:T(8,128)(2,1)S(1)}, bf16[144,384]{1,0:T(8,128)(2,1)S(1)}, u32[]{:S(2)}, u32[]{:S(2)}) collective-permute-start(bf16[144,384]{1,0:T(8,128)(2,1)S(1)} %get-tuple-element.34), channel_id=1, source_target_pairs={{1,2},{2,1},{3,4},{4,3},{5,6},{6,5},{7,8},{8,7},{9,10},{10,9},{11,... | collective-permute-start | bytes 331784 | tf_op jit(solution)/shard_map/ppermute | solution.py:569

commit v2 on v1

--- a/solution.py
+++ b/solution.py
@@ -80,11 +80,15 @@
     noise_hbm,
     context2_hbm,
     context1_hbm,
+    cand_hbm,
+    gates_hbm,
     hc_out,
     hf_out,
     noise_out,
     even_out,
     odd_out,
+    cand_out,
+    gates_out,
     frames,
     noise,
     context2,
@@ -106,7 +110,14 @@
             )
         )
     ]
-    for copy in moves:
+    weights = [
+        pltpu.make_async_copy(
+            cand_hbm.at[pl.ds(2 * C2 * t + C2, C2), :], cand_out.at[pl.ds(C2 * t, C2), :], sem.at[4 + t]
+        )
+        for t in range(TAPS)
+    ]
+    weights.append(pltpu.make_async_copy(gates_hbm, gates_out, sem.at[4 + TAPS]))
+    for copy in moves + weights:
         copy.start()
 
     def pick(shift, parity):
@@ -138,6 +149,21 @@
         both = dot_t(picks[4 - shift, 0], even) + dot_t(picks[4 - shift, 1], odd)
         return both.astype(BF16)
 
+    deep = turned(3)
+    left = jnp.concatenate(
+        [
+            jnp.concatenate([deep[32 * j : 32 * j + 32, 128 * r : 128 * r + 128] for r in range(RC)], 0)
+            for j in range(4)
+        ],
+        1,
+    )
+    moves[2].wait()
+    for q in range(2):
+        weight = dot_t(spreads[q], context1[...]).astype(BF16)
+        state1 = jnp.tanh(dot(left, weight)).astype(BF16)
+        for r in range(RC):
+            hf_out[2 * r + q] = state1[CF * r : CF * r + CF]
+
     deep = turned(4)
     left = jnp.concatenate(
         [
@@ -152,21 +178,6 @@
     weight = jnp.concatenate([moved[f][16 * j : 16 * j + 16] for j in range(16) for f in range(4)], 0)
     state2 = jnp.tanh(dot(left, weight))
     hc_out[...] = state2.astype(BF16).reshape(RC, CC, C2)
-
-    deep = turned(3)
-    left = jnp.concatenate(
-        [
-            jnp.concatenate([deep[32 * j : 32 * j + 32, 128 * r : 128 * r + 128] for r in range(RC)], 0)
-            for j in range(4)
-        ],
-        1,
-    )
-    moves[2].wait()
-    for q in range(2):
-        weight = dot_t(spreads[q], context1[...]).astype(BF16)
-        state1 = jnp.tanh(dot(left, weight)).astype(BF16)
-        for r in range(RC):
-            hf_out[2 * r + q] = state1[CF * r : CF * r + CF]
 
     moves[3].wait()
     diagonal = indicator(iota((16, 16), 0) == iota((16, 16), 1))
@@ -186,10 +197,12 @@
         buf[144:160, :] = jnp.zeros((16, C2), F32)
         buf[144:160, 0:128] = jnp.where(up, turned_noise, low_noise)
         target[...] = buf[...].astype(BF16)
+    for copy in weights:
+        copy.wait()
 
 
 def column_kernel(
-    place, hc, hf, noise, even_in, odd_in, after, ec_out, ef_out, en_out, even_out, odd_out, sc, sf, sn, buf
+    place, hc, hf, noise, odd_in, even_in, after, ec_out, ef_out, en_out, even_out, odd_out, sc, sf, sn, buf
 ):
     up_first = (place[0] & 1) == 1
     above = jnp.where(up_first, even_in[...].astype(F32), odd_in[...].astype(F32))
@@ -244,9 +257,8 @@
     inputs, states = [], []
     for hbm, held in ((gates_hbm, gates), (cand_hbm, cand)):
         inputs.append([move(hbm.at[pl.ds(2 * C2 * t, C2), :], held.at[t]) for t in range(TAPS)])
-    for hbm, target in ((gates_hbm, wg_out), (cand_hbm, wc_out)):
-        for t in range(TAPS):
-            states.append(move(hbm.at[pl.ds(2 * C2 * t + C2, C2), :], target.at[pl.ds(C2 * t, C2), :]))
+    for t in range(TAPS):
+        states.append(move(gates_hbm.at[pl.ds(2 * C2 * t + C2, C2), :], wg_out.at[pl.ds(C2 * t, C2), :]))
     acc_g[...] = jnp.zeros(acc_g.shape, F32)
     acc_c[...] = jnp.zeros(acc_c.shape, F32)
     first.wait()
@@ -257,13 +269,13 @@
             copies[t].wait()
             acc[8 * t : 8 * t + 8, :] = dot(wide, held[t])[0:8]
     wg_out[TAPS * C2 :, :] = acc_g[...].astype(BF16)
-    wc_out[TAPS * C2 :, :] = acc_c[...].astype(BF16)
+    wc_out[...] = acc_c[...].astype(BF16)
     for copy in states:
         copy.wait()
 
 
 def fine_weights_kernel(
-    after, gates_hbm, cand_hbm, up_hbm, head_hbm, wr_out, wu_out, wv_out, wc_out, up_out, head_out, gates, up, head, sem
+    after, gates, cand_hbm, up_hbm, head_hbm, wr_out, wu_out, wv_out, wc_out, up_out, head_out, up, head, sem
 ):
     moves = [
         pltpu.make_async_copy(src, dst, sem.at[i])
@@ -271,7 +283,6 @@
             (
                 (up_hbm, up),
                 (head_hbm, head),
-                (gates_hbm, gates),
                 (cand_hbm, wc_out.at[pl.ds(WF - C1, C1), :]),
             )
         )
@@ -290,14 +301,13 @@
     for i in range(4):
         part = jnp.concatenate([wide[:, C1 * i : C1 * i + C1], zeros], 1)
         up_out[:, 256 * i : 256 * i + 256] = part.astype(BF16)
-    moves[2].wait()
     for t in range(TAPS):
         rows = slice(2 * C1 * t, 2 * C1 * t + 2 * C1)
         part = gates[rows, 0:256].astype(F32)
         wr_out[rows, :] = jnp.concatenate([part[:, C1:256], part[:, :C1]], 1).astype(BF16)
         target, lane = (wv_out, 0) if t % 3 == 1 else (wu_out, 64 * (t % 3))
         target[2 * C1 * (t // 3) : 2 * C1 * (t // 3) + 2 * C1, lane : lane + 128] = gates[rows, 256:384]
-    moves[3].wait()
+    moves[2].wait()
 
 
 def main_kernel(
@@ -305,10 +315,11 @@
     ec,
     ef,
     en,
+    odd_in,
     even_in,
-    odd_in,
     wg2,
     wc2,
+    fold2,
     wr1,
     wu1,
     wv1,
@@ -410,7 +421,7 @@
         near = patch[QC * (first - 1) : QC * (first - 1 + rows), :].astype(BF16)
         return jnp.concatenate(taps(even_c, odd_c, QC, first, rows) + [near], 1)
 
-    def coarse_gates(step):
+    def coarse_ready(step):
         first, rows = 1 + 2 * step, 14 - 4 * step
         for t in range(3):
             if step == 0:
@@ -418,6 +429,9 @@
             else:
                 window = flat(next_h, t, QC)
             fill(even_c, odd_c, QC, 128 * t, first - 1, first + rows + 1, window)
+
+    def coarse_gates(step):
+        first, rows = 1 + 2 * step, 14 - 4 * step
         operand = coarse_left(first, rows)
         gates = dot(operand, wg2[:, 0:512])
         for t in range(3):
@@ -436,7 +450,7 @@
         operand = coarse_left(first, rows)
         good = valid(first, rows, QC, row0 * RC - HC, col0 * CC - 4, 1)
         for lanes, here in ((slice(0, 256), (0, 1)), (slice(256, 384), (2,))):
-            cand = jnp.tanh(dot(operand, wc2[:, lanes]))
+            cand = jnp.tanh(dot(operand, jnp.concatenate([wc2[:, lanes], fold2[:, lanes]], 0)))
             for i, t in enumerate(here):
                 new = cand[:, 128 * i : 128 * i + 128]
                 old = own_first(t, first, rows, 0) if step == 0 else cells(next_h, t, QC, first, rows)
@@ -470,10 +484,13 @@
         first, rows = 1 + 2 * step, 18 - 4 * step
         fill(even_f, odd_f, QF, 256, first - 1, first + rows + 1, flat(fine_h, 1, QF))
 
-    def fine_gates(step):
+    def fine_ready(step):
         first, rows = 1 + 2 * step, 18 - 4 * step
         fill(even_f, odd_f, QF, 0, first - 1, first + rows + 1, flat(fine_x, 0, QF))
         fine_mixed(fine_h, first - 1, first + rows + 1)
+
+    def fine_gates(step):
+        first, rows = 1 + 2 * step, 18 - 4 * step
         gates = dot(jnp.concatenate(taps(even_f, odd_f, QF, first, rows), 1), wr1[...])
         at = pl.ds(PAD + QF * first, QF * rows)
         gate = sigmoid(gates[:, 0:128])
@@ -488,10 +505,13 @@
         gate = dot(middle, wv1[...]) + side_u[0, pl.ds(PAD - 1, count), :] + side_u[1, pl.ds(PAD + 1, count), :]
         fine_u[1, pl.ds(PAD + QF * (first + 1), count), :] = sigmoid(gate)
 
-    def fine_cand():
+    def fine_cand_ready():
         first, rows = 2, 16
         fine_mixed(fine_reset, first - 1, first + rows + 1)
         fill(even_f, odd_f, QF, 256, first - 1, first + rows + 1, flat(fine_reset, 1, QF))
+
+    def fine_cand():
+        first, rows = 2, 16
         operand = jnp.concatenate(taps(even_f, odd_f, QF, first, rows), 1)
         good = valid(first, rows, QF, row0 * RC - HC + 3, col0 * CC - 2, 2)
         cand = jnp.tanh(dot_t(operand, wc1[...]))
@@ -543,18 +563,23 @@
         for t in range(2):
             out[step, :, 128 * t : 128 * t + 128] = final[:, t].reshape(8 * rows, 128)
 
+    coarse_ready(0)
     coarse_gates(0)
     fine_before(0)
     coarse_cand(0)
     fine_input(0)
+    coarse_ready(1)
     coarse_gates(1)
+    fine_ready(0)
     fine_gates(0)
     coarse_cand(1)
+    fine_cand_ready()
     fine_cand()
     fine_input(1)
+    fine_before(1)
+    fine_ready(1)
+    fine_gates(1)
     emit(0, jnp.concatenate([own_fine(fine_h, 0), own_fine(fine_h, 1)], 1).astype(BF16))
-    fine_before(1)
-    fine_gates(1)
     emit(1, fine_last())
 
 
@@ -599,7 +624,7 @@
     shape = jax.ShapeDtypeStruct
     row_buf, col_buf = shape((ROW_BUF, C2), BF16), shape((COL_BUF, C2), BF16)
 
-    hc, hf, noise, even, odd = call(
+    hc, hf, noise, even, odd, wc2, gates1 = call(
         start_kernel,
         [
             shape((RC, CC, C2), BF16),
@@ -607,8 +632,10 @@
             shape((16, 128), BF16),
             row_buf,
             row_buf,
-        ],
-        [SMEM] + [HBM] * 4,
+            shape((TAPS * C2, C2), BF16),
+            shape((18 * C1, 2 * C1), BF16),
+        ],
+        [SMEM] + [HBM] * 6,
         [
             pltpu.VMEM((4, 16 * RC, 16 * CC), BF16),
             pltpu.VMEM((RC, 8, CC), BF16),
@@ -618,22 +645,25 @@
             pltpu.VMEM((256, 256), BF16),
             pltpu.VMEM((2, 512, 256), BF16),
             pltpu.VMEM((ROW_BUF, C2), F32),
-            pltpu.SemaphoreType.DMA((4,)),
-        ],
-        16 << 20, 10**9, 2 << 20,
+            pltpu.SemaphoreType.DMA((5 + TAPS,)),
+        ],
+        16 << 20, 10**9, 8 << 20,
     )(
         place,
         in_hbm(context_frames),
         in_hbm(latent_noise.transpose(0, 2, 1)),
         in_hbm(coarse_context),
         in_hbm(fine_context.T),
+        in_hbm(coarse_candidate),
+        in_hbm(fine_gates),
     )
 
-    even, odd = swapped(even, "row", 0), swapped(odd, "row", 1)
-
-    wg2, wc2, token = call(
+    odd = swapped(odd, "row", 1)
+    even = swapped(even, "row", 0)
+
+    wg2, fold2, token = call(
         coarse_weights_kernel,
-        [shape((KC, 2 * C2), BF16), shape((KC, C2), BF16), shape((8, 128), F32)],
+        [shape((KC, 2 * C2), BF16), shape((128, C2), BF16), shape((8, 128), F32)],
         [HBM] * 3,
         [
             pltpu.VMEM((8, C2), BF16),
@@ -641,7 +671,7 @@
             pltpu.VMEM((TAPS, C2, C2), BF16),
             pltpu.VMEM((128, 2 * C2), F32),
             pltpu.VMEM((128, C2), F32),
-            pltpu.SemaphoreType.DMA((4 * TAPS + 1,)),
+            pltpu.SemaphoreType.DMA((3 * TAPS + 1,)),
         ],
         16 << 20, 10**9, 24 << 20,
     )(in_hbm(latent_proj), in_hbm(coarse_gates), in_hbm(coarse_candidate))
@@ -663,9 +693,10 @@
             pltpu.VMEM((COL_BUF, C2), F32),
         ],
         8 << 20, 10**6, 2 << 20,
-    )(place, hc, hf, noise, even, odd, token)
-
-    even, odd = swapped(even, "col", 0), swapped(odd, "col", 1)
+    )(place, hc, hf, noise, odd, even, token)
+
+    odd = swapped(odd, "col", 1)
+    even = swapped(even, "col", 0)
 
     wr1, wu1, wv1, wc1, up, head = call(
         fine_weights_kernel,
@@ -677,20 +708,19 @@
             shape((C2, 1024), BF16),
             shape((1024, WF), BF16),
         ],
-        [ANY] + [HBM] * 4,
-        [
-            pltpu.VMEM((18 * C1, 2 * C1), BF16),
+        [ANY, VMEM] + [HBM] * 3,
+        [
             pltpu.VMEM((C2, 4 * C1), BF16),
             pltpu.VMEM((64, C1), BF16),
             pltpu.SemaphoreType.DMA((4,)),
         ],
         12 << 20, 10**8, 8 << 20,
-    )(en, in_hbm(fine_gates), in_hbm(fine_candidate.T), in_hbm(upsample_proj), in_hbm(head_proj.T))
+    )(en, gates1, in_hbm(fine_candidate.T), in_hbm(upsample_proj), in_hbm(head_proj.T))
 
     (forecast,) = call(
         main_kernel,
         [shape((2, 96, 256), F32)],
-        [SMEM] + [VMEM] * 13,
+        [SMEM] + [VMEM] * 14,
         [
             pltpu.VMEM((3, EC * PC, 128), F32),
             pltpu.VMEM((EC * PC, 128), F32),
@@ -710,7 +740,7 @@
             pltpu.VMEM((3, (RF + 2) * CF, 2 * C1), BF16),
         ],
         26 << 20, 9 * 10**9, 30 << 20,
-    )(place, ec, ef, en, even, odd, wg2, wc2, wr1, wu1, wv1, wc1, up, head)
+    )(place, ec, ef, en, odd, even, wg2, wc2, fold2, wr1, wu1, wv1, wc1, up, head)
     return forecast
 
 

time: 41.9 us -> 40.8 us (0.974)
  the two profiles are of different devices: /device:TPU:19 before, /device:TPU:1 now
where the time goes in v2:
time: 40.8 us; the launch traced here: 40.6 us
  Pallas kernels  27.9 us (68%)
  starting transfers between devices  12.1 us (30%)
  waiting for transfers between devices  0.52 us (1%)
    pallas_call x1, Pallas kernels, on_device(): call(main_kernel, [shape((2, 96, 256), F32)], [SMEM] + [VMEM] * 14, [pltp...  16 us
    ppermute x4, starting transfers between devices, swapped(): return lax.ppermute(value, axis, pairs)  12.1 us
    pallas_call x1, Pallas kernels, on_device(): call(coarse_weights_kernel, [shape((KC, 2 * C2), BF16), shape((128, C2),...  5.02 us
    pallas_call x1, Pallas kernels, on_device(): call(start_kernel, [shape((RC, CC, C2), BF16), shape((RF, CF, WF), BF16),...  3.67 us
    pallas_call x1, Pallas kernels, on_device(): call(fine_weights_kernel, [shape((18 * C1, 256), BF16), shape((6 * C1, 25...  2.27 us
    pallas_call x1, Pallas kernels, on_device(): call(column_kernel, [shape((EC, CC, C2), BF16), shape((EF, CF, WF), BF16)...  0.96 us
  transfers between devices with their start and end apart: 4, of which 2 were waited for; matrix products, arithmetic and copies ran while one was open for 0% of the time, Pallas kernels for 18%

profile of v2, /device:TPU:1, one launch (start us, length us, event | category | flops | bytes accessed | tf_op | source)
XLA Modules:
  0.0 40.6 jit_solution(2424384087270133227)
XLA Ops:
  0.0 0.1 pad_add_fusion.place
  0.1 3.7 %shard_map.109 = (bf16[6,16,384]{2,1,0:T(8,128)(2,1)S(1)}, bf16[12,32,256]{2,1,0:T(8,128)(2,1)S(1)}, bf16[16,128]{1,0:T(8,128)(2,1)S(1)}, bf16[160,384]{1,0:T(8,...) custom-call(s32[2]{0:T(128)S(1)} %pad_add_fusion.place, ...), custom_call_target="tpu_custom_call" | custom-call | flops 1000000000 | bytes 8388608 | tf_op jit(solution)/shard_map/pallas_call | solution.py:627
  3.8 0.7 %collective-permute-start = (bf16[160,384]{1,0:T(8,128)(2,1)S(1)}, bf16[160,384]{1,0:T(8,128)(2,1)S(1)}, u32[]{:S(2)}, u32[]{:S(2)}) collective-permute-start(bf16[160,384]{1,0:T(8,128)(2,1)S(1)} %get-tuple-element.29), channel_id=1, source_target_pairs={{16,32},{32,16},{48,64},{64,48},{80,96},{96,80},{17,33},{33,17},{4... | collective-permute-start | bytes 368648 | tf_op jit(solution)/shard_map/ppermute | solution.py:594
  4.4 6.5 %collective-permute-start.1 = (bf16[160,384]{1,0:T(8,128)(2,1)S(1)}, bf16[160,384]{1,0:T(8,128)(2,1)S(1)}, u32[]{:S(2)}, u32[]{:S(2)}) collective-permute-start(bf16[160,384]{1,0:T(8,128)(2,1)S(1)} %get-tuple-element.30), channel_id=1, source_target_pairs={{0,16},{16,0},{32,48},{48,32},{64,80},{80,64},{96,112},{112,96},{1... | collective-permute-start | bytes 368648 | tf_op jit(solution)/shard_map/ppermute | solution.py:594
  10.9 5.0 %shard_map.110 = (bf16[3584,768]{1,0:T(8,128)(2,1)S(1)}, bf16[128,384]{1,0:T(8,128)(2,1)S(1)}, f32[8,128]{1,0:T(8,128)S(1)}) custom-call(bf16[8,384]{1,0:T(8,128)(2,1)} %proj_hbm.1, bf16[6912,768]{1,0:T(8,128)(2,1)} %gates_hbm.3, bf16[6912,384]{1,0:T(8,128)(2,1)} %cand_hbm.3), custom_call_target="tpu_custom_call" | custom-call | flops 1000000000 | bytes 25165824 | tf_op jit(solution)/shard_map/pallas_call | solution.py:664
  15.9 0.0 collective-permute-done.odd_in
  16.0 0.2 collective-permute-done.1.even_in
  16.2 1.0 %shard_map.111 = (bf16[16,16,384]{2,1,0:T(8,128)(2,1)S(1)}, bf16[20,32,256]{2,1,0:T(8,128)(2,1)S(1)}, bf16[16,16,128]{2,1,0:T(8,128)(2,1)S(1)}, bf16[144,384]{1,0:T(8,128)(2,1)S(1)}, bf16[144,384]{1,0:T(8,128)(2,1)S(1)}) custom-call(s32[2]{0:T(128)S(1)} %pad_add_fusion.place, bf16[6,16,384]{2,1,0:T(8,128)(2,1)S(1)} %get-tuple-element.26.hc, ...), custom_call_target="tpu_custom_call" | custom-call | flops 1000000 | bytes 2097152 | tf_op jit(solution)/shard_map/pallas_call | solution.py:679
  17.1 4.6 %collective-permute-start.2 = (bf16[144,384]{1,0:T(8,128)(2,1)S(1)}, bf16[144,384]{1,0:T(8,128)(2,1)S(1)}, u32[]{:S(2)}, u32[]{:S(2)}) collective-permute-start(bf16[144,384]{1,0:T(8,128)(2,1)S(1)} %get-tuple-element.35), channel_id=1, source_target_pairs={{1,2},{2,1},{3,4},{4,3},{5,6},{6,5},{7,8},{8,7},{9,10},{10,9},{11,... | collective-permute-start | bytes 331784 | tf_op jit(solution)/shard_map/ppermute | solution.py:594
  21.8 0.3 collective-permute-start.3
  22.1 2.3 %shard_map.112 = (bf16[3456,256]{1,0:T(8,128)(2,1)S(1)}, bf16[1152,256]{1,0:T(8,128)(2,1)S(1)}, bf16[1152,128]{1,0:T(8,128)(2,1)S(1)}, bf16[256,3456]{1,0:T(8,12...) custom-call(bf16[16,16,128]{2,1,0:T(8,128)(2,1)S(1)} %get-tuple-element.34.after.en, ...), custom_call_target="tpu_custom_call" | custom-call | flops 100000000 | bytes 8388608 | tf_op jit(solution)/shard_map/pallas_call | solution.py:701
  24.3 0.3 collective-permute-done.2.odd_in
  24.6 0.0 collective-permute-done.3.even_in
  24.6 16.0 %shard_map.113 = f32[2,96,256]{2,1,0:T(8,128)} custom-call(s32[2]{0:T(128)S(1)} %pad_add_fusion.place, bf16[16,16,384]{2,1,0:T(8,128)(2,1)S(1)} %get-tuple-element.32.ec, bf16[20,32,256]{2,1,0:T(8,128)(2,1)S(1)} %get-tuple-element.33.ef, bf16[16,16,128]{2,1,0:T(8,128)(2,1)S(1)} %get-tuple-element.34.after.en, ...), custom_call_target="tpu_custom_call" | custom-call | flops 8999999488 | bytes 31457280 | tf_op jit(solution)/shard_map/pallas_call | solution.py:720
Async XLA Ops:
  3.8 12.2 %collective-permute-start = (bf16[160,384]{1,0:T(8,128)(2,1)S(1)}, bf16[160,384]{1,0:T(8,128)(2,1)S(1)}, u32[]{:S(2)}, u32[]{:S(2)}) collective-permute-start(bf16[160,384]{1,0:T(8,128)(2,1)S(1)} %get-tuple-element.29), channel_id=1, source_target_pairs={{16,32},{32,16},{48,64},{64,48},{80,96},{96,80},{17,33},{33,17},{4... | collective-permute-start | bytes 368648 | tf_op jit(solution)/shard_map/ppermute | solution.py:594
  4.4 11.7 %collective-permute-start.1 = (bf16[160,384]{1,0:T(8,128)(2,1)S(1)}, bf16[160,384]{1,0:T(8,128)(2,1)S(1)}, u32[]{:S(2)}, u32[]{:S(2)}) collective-permute-start(bf16[160,384]{1,0:T(8,128)(2,1)S(1)} %get-tuple-element.30), channel_id=1, source_target_pairs={{0,16},{16,0},{32,48},{48,32},{64,80},{80,64},{96,112},{112,96},{1... | collective-permute-start | bytes 368648 | tf_op jit(solution)/shard_map/ppermute | solution.py:594
  17.1 7.5 %collective-permute-start.2 = (bf16[144,384]{1,0:T(8,128)(2,1)S(1)}, bf16[144,384]{1,0:T(8,128)(2,1)S(1)}, u32[]{:S(2)}, u32[]{:S(2)}) collective-permute-start(bf16[144,384]{1,0:T(8,128)(2,1)S(1)} %get-tuple-element.35), channel_id=1, source_target_pairs={{1,2},{2,1},{3,4},{4,3},{5,6},{6,5},{7,8},{8,7},{9,10},{10,9},{11,... | collective-permute-start | bytes 331784 | tf_op jit(solution)/shard_map/ppermute | solution.py:594
  21.8 2.9 %collective-permute-start.3 = (bf16[144,384]{1,0:T(8,128)(2,1)S(1)}, bf16[144,384]{1,0:T(8,128)(2,1)S(1)}, u32[]{:S(2)}, u32[]{:S(2)}) collective-permute-start(bf16[144,384]{1,0:T(8,128)(2,1)S(1)} %get-tuple-element.36), channel_id=1, source_target_pairs={{0,1},{1,0},{2,3},{3,2},{4,5},{5,4},{6,7},{7,6},{8,9},{9,8},{10,11... | collective-permute-start | bytes 331784 | tf_op jit(solution)/shard_map/ppermute | solution.py:594

commit v3 on v2

--- a/solution.py
+++ b/solution.py
@@ -202,7 +202,7 @@
 
 
 def column_kernel(
-    place, hc, hf, noise, odd_in, even_in, after, ec_out, ef_out, en_out, even_out, odd_out, sc, sf, sn, buf
+    place, hc, hf, noise, even_in, odd_in, after, ec_out, ef_out, en_out, even_out, odd_out, sc, sf, sn, buf
 ):
     up_first = (place[0] & 1) == 1
     above = jnp.where(up_first, even_in[...].astype(F32), odd_in[...].astype(F32))
@@ -567,13 +567,13 @@
     coarse_gates(0)
     fine_before(0)
     coarse_cand(0)
+    coarse_ready(1)
     fine_input(0)
-    coarse_ready(1)
     coarse_gates(1)
     fine_ready(0)
     fine_gates(0)
+    fine_cand_ready()
     coarse_cand(1)
-    fine_cand_ready()
     fine_cand()
     fine_input(1)
     fine_before(1)
@@ -693,7 +693,7 @@
             pltpu.VMEM((COL_BUF, C2), F32),
         ],
         8 << 20, 10**6, 2 << 20,
-    )(place, hc, hf, noise, odd, even, token)
+    )(place, hc, hf, noise, even, odd, token)
 
     odd = swapped(odd, "col", 1)
     even = swapped(even, "col", 0)

time: 40.8 us -> 40.3 us (0.988)
  the two profiles are of different devices: /device:TPU:1 before, /device:TPU:19 now
where the time goes in v3:
time: 40.3 us; the launch traced here: 39.9 us
  Pallas kernels  27.9 us (69%)
  starting transfers between devices  10.6 us (26%)
  waiting for transfers between devices  1.27 us (3%)
    pallas_call x1, Pallas kernels, on_device(): call(main_kernel, [shape((2, 96, 256), F32)], [SMEM] + [VMEM] * 14, [pltp...  16 us
    ppermute x4, starting transfers between devices, swapped(): return lax.ppermute(value, axis, pairs)  10.6 us
    pallas_call x1, Pallas kernels, on_device(): call(coarse_weights_kernel, [shape((KC, 2 * C2), BF16), shape((128, C2),...  5.03 us
    pallas_call x1, Pallas kernels, on_device(): call(start_kernel, [shape((RC, CC, C2), BF16), shape((RF, CF, WF), BF16),...  3.67 us
    pallas_call x1, Pallas kernels, on_device(): call(fine_weights_kernel, [shape((18 * C1, 256), BF16), shape((6 * C1, 25...  2.27 us
    ppermute x4, waiting for transfers between devices, swapped(): return lax.ppermute(value, axis, pairs)  1.27 us
    pallas_call x1, Pallas kernels, on_device(): call(column_kernel, [shape((EC, CC, C2), BF16), shape((EF, CF, WF), BF16)...  0.97 us
  transfers between devices with their start and end apart: 4, of which 1 were waited for; matrix products, arithmetic and copies ran while one was open for 0% of the time, Pallas kernels for 18%

profile of v3, /device:TPU:19, one launch (start us, length us, event | category | flops | bytes accessed | tf_op | source)
XLA Modules:
  0.0 39.9 jit_solution(2005029195123766868)
XLA Ops:
  0.0 0.1 pad_add_fusion.place
  0.1 3.7 %shard_map.109 = (bf16[6,16,384]{2,1,0:T(8,128)(2,1)S(1)}, bf16[12,32,256]{2,1,0:T(8,128)(2,1)S(1)}, bf16[16,128]{1,0:T(8,128)(2,1)S(1)}, bf16[160,384]{1,0:T(8,...) custom-call(s32[2]{0:T(128)S(1)} %pad_add_fusion.place, ...), custom_call_target="tpu_custom_call" | custom-call | flops 1000000000 | bytes 8388608 | tf_op jit(solution)/shard_map/pallas_call | solution.py:627
  3.8 0.1 collective-permute-start
  3.9 6.2 %collective-permute-start.1 = (bf16[160,384]{1,0:T(8,128)(2,1)S(1)}, bf16[160,384]{1,0:T(8,128)(2,1)S(1)}, u32[]{:S(2)}, u32[]{:S(2)}) collective-permute-start(bf16[160,384]{1,0:T(8,128)(2,1)S(1)} %get-tuple-element.30), channel_id=1, source_target_pairs={{16,32},{32,16},{48,64},{64,48},{80,96},{96,80},{17,33},{33,17},{4... | collective-permute-start | bytes 368648 | tf_op jit(solution)/shard_map/ppermute | solution.py:594
  10.1 5.0 %shard_map.110 = (bf16[3584,768]{1,0:T(8,128)(2,1)S(1)}, bf16[128,384]{1,0:T(8,128)(2,1)S(1)}, f32[8,128]{1,0:T(8,128)S(1)}) custom-call(bf16[8,384]{1,0:T(8,128)(2,1)} %proj_hbm.1, bf16[6912,768]{1,0:T(8,128)(2,1)} %gates_hbm.3, bf16[6912,384]{1,0:T(8,128)(2,1)} %cand_hbm.3), custom_call_target="tpu_custom_call" | custom-call | flops 1000000000 | bytes 25165824 | tf_op jit(solution)/shard_map/pallas_call | solution.py:664
  15.1 0.0 collective-permute-done.even_in
  15.1 0.0 collective-permute-done.1.odd_in
  15.1 1.0 %shard_map.111 = (bf16[16,16,384]{2,1,0:T(8,128)(2,1)S(1)}, bf16[20,32,256]{2,1,0:T(8,128)(2,1)S(1)}, bf16[16,16,128]{2,1,0:T(8,128)(2,1)S(1)}, bf16[144,384]{1,0:T(8,128)(2,1)S(1)}, bf16[144,384]{1,0:T(8,128)(2,1)S(1)}) custom-call(s32[2]{0:T(128)S(1)} %pad_add_fusion.place, bf16[6,16,384]{2,1,0:T(8,128)(2,1)S(1)} %get-tuple-element.26.hc, ...), custom_call_target="tpu_custom_call" | custom-call | flops 1000000 | bytes 2097152 | tf_op jit(solution)/shard_map/pallas_call | solution.py:679
  16.1 4.0 %collective-permute-start.2 = (bf16[144,384]{1,0:T(8,128)(2,1)S(1)}, bf16[144,384]{1,0:T(8,128)(2,1)S(1)}, u32[]{:S(2)}, u32[]{:S(2)}) collective-permute-start(bf16[144,384]{1,0:T(8,128)(2,1)S(1)} %get-tuple-element.35), channel_id=1, source_target_pairs={{1,2},{2,1},{3,4},{4,3},{5,6},{6,5},{7,8},{8,7},{9,10},{10,9},{11,... | collective-permute-start | bytes 331784 | tf_op jit(solution)/shard_map/ppermute | solution.py:594
  20.1 0.3 collective-permute-start.3
  20.4 2.3 %shard_map.112 = (bf16[3456,256]{1,0:T(8,128)(2,1)S(1)}, bf16[1152,256]{1,0:T(8,128)(2,1)S(1)}, bf16[1152,128]{1,0:T(8,128)(2,1)S(1)}, bf16[256,3456]{1,0:T(8,12...) custom-call(bf16[16,16,128]{2,1,0:T(8,128)(2,1)S(1)} %get-tuple-element.34.after.en, ...), custom_call_target="tpu_custom_call" | custom-call | flops 100000000 | bytes 8388608 | tf_op jit(solution)/shard_map/pallas_call | solution.py:701
  22.7 1.3 %collective-permute-done.2.odd_in = bf16[144,384]{1,0:T(8,128)(2,1)S(1)} collective-permute-done((bf16[144,384]{1,0:T(8,128)(2,1)S(1)}, bf16[144,384]{1,0:T(8,128)(2,1)S(1)}, u32[]{:S(2)}, u32[]{:S(2)}) %collective-permute-start.2) | collective-permute-done | bytes 110624 | tf_op jit(solution)/shard_map/ppermute | solution.py:594
  24.0 0.0 collective-permute-done.3.even_in
  24.0 16.0 %shard_map.113 = f32[2,96,256]{2,1,0:T(8,128)} custom-call(s32[2]{0:T(128)S(1)} %pad_add_fusion.place, bf16[16,16,384]{2,1,0:T(8,128)(2,1)S(1)} %get-tuple-element.32.ec, bf16[20,32,256]{2,1,0:T(8,128)(2,1)S(1)} %get-tuple-element.33.ef, bf16[16,16,128]{2,1,0:T(8,128)(2,1)S(1)} %get-tuple-element.34.after.en, ...), custom_call_target="tpu_custom_call" | custom-call | flops 8999999488 | bytes 31457280 | tf_op jit(solution)/shard_map/pallas_call | solution.py:720
Async XLA Ops:
  3.8 11.4 %collective-permute-start = (bf16[160,384]{1,0:T(8,128)(2,1)S(1)}, bf16[160,384]{1,0:T(8,128)(2,1)S(1)}, u32[]{:S(2)}, u32[]{:S(2)}) collective-permute-start(bf16[160,384]{1,0:T(8,128)(2,1)S(1)} %get-tuple-element.29), channel_id=1, source_target_pairs={{0,16},{16,0},{32,48},{48,32},{64,80},{80,64},{96,112},{112,96},{1... | collective-permute-start | bytes 368648 | tf_op jit(solution)/shard_map/ppermute | solution.py:594
  3.9 11.2 %collective-permute-start.1 = (bf16[160,384]{1,0:T(8,128)(2,1)S(1)}, bf16[160,384]{1,0:T(8,128)(2,1)S(1)}, u32[]{:S(2)}, u32[]{:S(2)}) collective-permute-start(bf16[160,384]{1,0:T(8,128)(2,1)S(1)} %get-tuple-element.30), channel_id=1, source_target_pairs={{16,32},{32,16},{48,64},{64,48},{80,96},{96,80},{17,33},{33,17},{4... | collective-permute-start | bytes 368648 | tf_op jit(solution)/shard_map/ppermute | solution.py:594
  16.1 7.9 %collective-permute-start.2 = (bf16[144,384]{1,0:T(8,128)(2,1)S(1)}, bf16[144,384]{1,0:T(8,128)(2,1)S(1)}, u32[]{:S(2)}, u32[]{:S(2)}) collective-permute-start(bf16[144,384]{1,0:T(8,128)(2,1)S(1)} %get-tuple-element.35), channel_id=1, source_target_pairs={{1,2},{2,1},{3,4},{4,3},{5,6},{6,5},{7,8},{8,7},{9,10},{10,9},{11,... | collective-permute-start | bytes 331784 | tf_op jit(solution)/shard_map/ppermute | solution.py:594
  20.1 3.8 %collective-permute-start.3 = (bf16[144,384]{1,0:T(8,128)(2,1)S(1)}, bf16[144,384]{1,0:T(8,128)(2,1)S(1)}, u32[]{:S(2)}, u32[]{:S(2)}) collective-permute-start(bf16[144,384]{1,0:T(8,128)(2,1)S(1)} %get-tuple-element.36), channel_id=1, source_target_pairs={{0,1},{1,0},{2,3},{3,2},{4,5},{5,4},{6,7},{7,6},{8,9},{9,8},{10,11... | collective-permute-start | bytes 331784 | tf_op jit(solution)/shard_map/ppermute | solution.py:594
